TPU v7x, 128 devices: a whole 4x4x4 slice. The times are simulated.
128 devices in a mesh: lat: 8 (over z, x_hi), lon: 16 (over y, x_lo, core).
Axes of the slice: x: 4 (x_hi: 2, x_lo: 2; x = x_hi * 2 + x_lo), y: 4, z: 4, core: 2. Of those that a mesh axis runs over, the one named last changes fastest.
Arguments:
- grid_inputs: bfloat16 [8, 16, 1024, 474], P('lat', 'lon'), may hold values from -6 to 6
- mesh_state: bfloat16 [8, 16, 128, 512], P('lat', 'lon'), may hold values from -6 to 6
- embed_in: bfloat16 [474, 512], replicated, may hold values from -0.25 to 0.25
- embed_out: bfloat16 [512, 512], replicated, may hold values from -0.25 to 0.25
- edge_square: bfloat16 [3, 3, 512, 512], replicated, may hold values from -0.25 to 0.25
- edge_geom_weight: float32 [3, 4, 512], replicated, may hold values from -3 to 3
- node_first: bfloat16 [3, 1024, 512], replicated, may hold values from -0.1875 to 0.1875
- node_second: bfloat16 [2, 512, 512], replicated, may hold values from -0.25 to 0.25
- head: bfloat16 [512, 227], replicated, may hold values from -0.25 to 0.25
- g2m_senders: int32 [8, 16, 2048], P('lat', 'lon'), may hold values from 0 to 9215, as said below
- g2m_receivers: int32 [8, 16, 2048], P('lat', 'lon'), may hold values from 0 to 127
- g2m_counts: int32 [8, 16], P('lat', 'lon'), may hold values from 1024 to 2048, as said below
- g2m_geom: float32 [8, 16, 4, 2048], P('lat', 'lon'), may hold values from -6 to 6
- mesh_senders: int32 [8, 16, 768], P('lat', 'lon'), may hold values from 0 to 1151, as said below
- mesh_geom: float32 [8, 16, 4, 768], P('lat', 'lon'), may hold values from -6 to 6
- coarse_senders: int32 [8, 16, 256], P('lat', 'lon'), may hold values from 0 to 2047
- coarse_receivers: int32 [8, 16, 256], P('lat', 'lon'), may hold values from 0 to 2047, as said below
- coarse_geom: float32 [8, 16, 4, 256], P('lat', 'lon'), may hold values from -6 to 6
- m2g_senders: int32 [8, 16, 3072], P('lat', 'lon'), may hold values from 0 to 1151, as said below
- m2g_geom: float32 [8, 16, 4, 3072], P('lat', 'lon'), may hold values from -6 to 6
Outputs:
- grid_outputs: bfloat16 [8, 16, 1024, 227], P('lat', 'lon')
Inputs may be any that keep to these rules, and one draw needn't show every extreme that they name: `g2m_senders`: index s names node s % 1024 of neighbour s // 1024 of the tile; never a neighbour beyond the first or last band. `mesh_senders`: index s names node s % 128 of neighbour s // 128 of the tile; never a neighbour beyond the first or last band. `m2g_senders`: index s names node s % 128 of neighbour s // 128 of the tile; never a neighbour beyond the first or last band. `g2m_counts`: sector 0 of the first and last bands uses all 2048 slots; sector 0 of the band or bands farthest from both ends uses 2048 // 2. `coarse_receivers`: an edge of a tile enters a coarse node of that tile, of the tile before it in the numbering (counted round), or of the tile half the numbering away.
All inputs are finite; a program needn't handle non-finite values.
Results may differ from a plain program's by a relative error of at most 0.019.
Values may be sent and summed in bfloat16 or wider, within the bound.
No kernel may reach another device: no remote copies, remote signals or barrier semaphores. Data moves between devices by JAX's collectives and lax.ppermute only.
A program may use at most 128 MiB of HBM per device.

v0:
```python
import functools

import jax
import jax.numpy as jnp
from jax import lax
from jax.experimental import pallas as pl
from jax.experimental.pallas import tpu as pltpu
from jax.sharding import PartitionSpec as P

BF = jnp.bfloat16
F32 = jnp.float32
I32 = jnp.int32
WIDTH = 512
GRID_NODES = 1024
MESH_NODES = 128
MESH_DEGREE = 6
GRID_DEGREE = 3
COARSE_DEV = 16
SLOTS = 2048
CHUNK = 512
CHUNKS = SLOTS // CHUNK
LISTED = MESH_NODES + 8 * CHUNKS
PAYLOAD = LISTED + 16
COARSE_EDGES = 256
LON = 16
NEAR_SLOTS = 160
COARSE_SLOTS = 320
GROUPS = (5, 3, 7, 0, 1, 2, 6, 4, 8)
VMEM_BYTES = 14 * 1024 * 1024


def mm(left, right):
    return jnp.dot(left, right, preferred_element_type=F32)


def mm_t(left, right):
    return lax.dot_general(left, right, (((0,), (0,)), ((), ())), preferred_element_type=F32)


def mm_nt(left, right):
    return lax.dot_general(left, right, (((1,), (1,)), ((), ())), preferred_element_type=F32)


def silu(v):
    half = 0.5 * v
    return half + half * jnp.tanh(half)


def one_hot(column, width):
    spots = lax.broadcasted_iota(I32, (column.shape[0], width), 1)
    return jnp.where(spots == column, 1.0, 0.0).astype(BF)


class Load:
    def __init__(self, index, shape):
        self.index, self.shape = index, shape


class View:
    def __init__(self, index):
        self.index = index


class Arriving:
    def __init__(self, copy, ref):
        self.copy, self.ref = copy, ref
        self.shape = ref.shape

    def ready(self):
        if self.copy is not None:
            self.copy.wait()
            self.copy = None
        return self.ref

    def __getitem__(self, index):
        return self.ready()[index]


V = pl.BlockSpec(memory_space=pltpu.VMEM)
SMEM = pl.BlockSpec(memory_space=pltpu.SMEM)
ANY = pl.BlockSpec(memory_space=pl.ANY)
HBM = pl.BlockSpec(memory_space=pltpu.HBM)


def square(block, kind):
    return Load((block, kind), (WIDTH, WIDTH))


def first_half(block, half):
    return Load((block, slice(WIDTH * half, WIDTH * (half + 1))), (WIDTH, WIDTH))


def second_of(block):
    return Load((block,), (WIDTH, WIDTH))


KEPT = (
    ("first", first_half(0, 0)), ("second", second_of(0)), ("square", square(1, 0)), ("square", square(1, 1)),
    ("first", first_half(1, 0)), ("second", second_of(1)), ("square", square(2, 0)),
)
ENCODER = (square(0, 0),)


def kernel_call(body, outs, specs, args, scratch=(), flops=0, moved=0, name=None, out_specs=None):
    loads = [(k, spec, args[k].dtype) for k, spec in enumerate(specs) if isinstance(spec, Load)]
    n_in, n_loads = len(specs), len(loads)

    def run(*refs):
        given, rest = list(refs[:n_in]), list(refs[n_in:])
        if n_loads:
            sems = rest[-1]
            buffers = rest[-1 - n_loads : -1]
            rest = rest[: -1 - n_loads]
            for at, ((k, spec, _), buffer) in enumerate(zip(loads, buffers)):
                source = given[k].at[spec.index] if spec.index else given[k]
                copy = pltpu.make_async_copy(source, buffer, sems.at[at])
                copy.start()
                given[k] = Arriving(copy, buffer)
        for k, spec in enumerate(specs):
            if isinstance(spec, View):
                given[k] = given[k].at[spec.index]
        body(*given, *rest)
        for part in given:
            if isinstance(part, Arriving):
                part.ready()

    extra = [pltpu.VMEM(spec.shape, dtype) for _, spec, dtype in loads]
    if loads:
        extra.append(pltpu.SemaphoreType.DMA((n_loads,)))
    many = isinstance(outs, tuple)
    args = [
        pltpu.with_memory_space_constraint(arg, pltpu.HBM) if spec is HBM or isinstance(spec, Load) else arg
        for spec, arg in zip(specs, args)
    ]
    return pl.pallas_call(
        run,
        out_shape=outs,
        in_specs=[HBM if isinstance(q, Load) else V if isinstance(q, View) else q for q in specs],
        out_specs=out_specs if out_specs is not None else (V,) * len(outs) if many else V,
        scratch_shapes=list(scratch) + extra,
        compiler_params=pltpu.CompilerParams(vmem_limit_bytes=VMEM_BYTES),
        cost_estimate=pl.CostEstimate(flops=flops, bytes_accessed=moved, transcendentals=0),
        name=name,
    )(*args)


def shaped(shape, dtype):
    return jax.ShapeDtypeStruct(shape, dtype)


def fill_list(scr, width, indices, geometry):
    for row, value in enumerate(indices):
        scr[row : row + 1, 0:width] = value.astype(F32)
    high = geometry.astype(BF).astype(F32)
    scr[4:8, 0:width] = high
    scr[8:12, 0:width] = geometry - high
    scr[12:16, 0:width] = high


def pack_body(
    count, senders, receivers, geometry, state, c_senders, c_receivers, c_geometry, weight,
    out, own, coarse, w_out, scr, short,
):
    for c in range(CHUNKS):
        cols = slice(c * CHUNK, (c + 1) * CHUNK)
        s = senders[:, cols]
        edge = lax.broadcasted_iota(I32, (1, CHUNK), 1) + c * CHUNK
        code = jnp.where(edge < count[0, 0], lax.shift_right_logical(s, 10) + 1, 0)
        local = s & (GRID_NODES - 1)
        fill_list(
            scr, CHUNK, (code, lax.shift_right_logical(local, 8), local & 255, receivers[:, cols]), geometry[:, cols]
        )
        own[16 * c : 16 * (c + 1), :] = scr[...].astype(BF)
        short[8 * c : 8 * (c + 1), :] = scr[0:8, :]
    out[MESH_NODES:LISTED, :] = short[...].astype(BF)
    s = c_senders[...]
    r = c_receivers[...]
    n = s.shape[1]
    fill_list(
        scr, n, (lax.shift_right_logical(s, 8), s & 255, lax.shift_right_logical(r, 4), r & 15), c_geometry[...]
    )
    out[LISTED:PAYLOAD, :] = scr[...].astype(BF)
    coarse[...] = scr[:, 0:n].astype(BF)
    zero = jnp.zeros((4, WIDTH), F32)
    for k in range(3):
        w = weight[k]
        high = w.astype(BF).astype(F32)
        scr[0:4, :] = zero
        scr[4:8, :] = high
        scr[8:12, :] = high
        scr[12:16, :] = w - high
        w_out[k] = scr[...].astype(BF)
        if k == 0:
            scr[8:12, :] = zero
            w_out[3] = scr[...].astype(BF)
    out[0:MESH_NODES, :] = state[...]


def prep_body(m_senders, m_geometry, d_senders, d_geometry, left, right, order, *refs):
    n = len(KEPT)
    sources, (m_out, d_out, o_left, o_right) = refs[:n], refs[n : n + 4]
    kept, (scr, turned, sems) = refs[n + 4 : -3], refs[-3:]
    o_left[...] = left[...]
    o_right[...] = right[...]
    copies = bring(sources, [load for _, load in KEPT], kept, sems)
    for senders, geometry, degree, out in (
        (m_senders, m_geometry, MESH_DEGREE, m_out),
        (d_senders, d_geometry, GRID_DEGREE, d_out),
    ):
        n = senders.shape[1]
        s = senders[...]
        near = lax.shift_right_logical(s, 7)
        spot = jnp.zeros_like(near)
        for place, group in enumerate(GROUPS):
            spot = jnp.where(near == place, group, spot)
        spot = spot * MESH_NODES + (s & (MESH_NODES - 1))
        zero = jnp.zeros((1, n), F32)
        fill_list(scr, n, (spot, zero, zero, zero), geometry[...])
        turned[0:n, :] = scr[:, 0:n].T
        for t in range(degree):
            out[t] = turned[pl.ds(t, n // degree, stride=degree), :]
    for copy in copies:
        copy.wait()


def embed_body(x, w_in, w_out, source, latent, w_send, sems):
    copies = bring((source,), ENCODER, (w_send,), sems)
    x, w_in, w_out = x.ready(), w_in.ready(), w_out.ready()

    @pl.loop(0, 4)
    def _(b):
        rows = pl.ds(pl.multiple_of(256 * b, 256), 256)
        hidden = silu(mm_t(x[:, rows], w_in[...])).astype(BF)
        latent[rows, :] = mm(hidden, w_out[...]).astype(BF)

    for copy in copies:
        copy.wait()


def send_body(latent, w_send, order, order_too, send):
    @pl.loop(0, 2)
    def _(b):
        rows = pl.ds(pl.multiple_of(512 * b, 512), 512)
        send[rows, :] = mm(latent[rows, :], w_send[...]).astype(BF)


def grid_body(latent, w_recv, w_first, order, recv, base):
    w_recv, w_first = w_recv.ready(), w_first.ready()

    @pl.loop(0, 4)
    def _(b):
        rows = pl.ds(pl.multiple_of(256 * b, 256), 256)
        recv[rows, :] = mm(latent[rows, :], w_recv[...]).astype(BF)
        base[rows, :] = mm(latent[rows, :], w_first[...])


def bring(sources, loads, outs, sems):
    copies = []
    for k, load in enumerate(loads):
        copies.append(pltpu.make_async_copy(sources[k].at[load.index], outs[k], sems.at[k]))
        copies[-1].start()
    return copies


def fold_body(*refs):
    for k in range(3):
        refs[7 + k][...] = mm(refs[2 * k][...], refs[2 * k + 1][...]).astype(BF)


def self_body(chunks, state, listed, send, w_recv, w_geom, *refs):
    total = jnp.zeros((MESH_NODES, WIDTH), F32) if len(refs) == 1 else refs[0][...]
    if len(refs) == 2 and refs[1].shape == (32, WIDTH):
        refs[1][...] = listed[32:64, :]
        out = refs[0]
        total = jnp.zeros((MESH_NODES, WIDTH), F32)
    else:
        out = refs[-1]
    q = None
    for c in chunks:
        d = listed[16 * c : 16 * (c + 1), :].astype(F32).T
        s = (d[:, 1:2] * 256.0 + d[:, 2:3]).astype(I32)
        r = jnp.where(d[:, 0:1] == 5.0, d[:, 3:4], -1.0).astype(I32)
        pick = one_hot(r, MESH_NODES)
        pre = mm(one_hot(s, GRID_NODES), send[...]) + mm(d.astype(BF), w_geom[...])
        if q is None:
            q = mm(state[...], w_recv[...]).astype(BF)
        total += mm_t(pick, silu(pre + mm(pick, q)).astype(BF))
    out[...] = total


def near_body(buckets, place, *refs):
    sources, refs = refs[: len(buckets)], refs[len(buckets) :]
    if len(refs) == 16:
        beside, order_first, order_last, *refs = refs
    send, w_recv, w_geom, *refs = refs
    outs, refs = refs[: len(buckets)], refs[len(buckets) :]
    if len(refs) == 6 and buckets[0] != 5:
        following, *refs = refs
        n = COARSE_EDGES
        last = (place[0, 4] & (LON - 1)) == LON - 1
        following[...] = jnp.where(
            last, sources[-1][LISTED:PAYLOAD, 0:n].astype(F32), beside[...].astype(F32)
        ).astype(BF)
    if len(buckets) == 4 and buckets[0] == 5:
        following, *refs = refs
        following[...] = sources[1][LISTED:PAYLOAD, 0:COARSE_EDGES]
    masks, ranks, q, edges, sums = refs
    band = lax.shift_right_logical(place[0, 4], 4)
    lists = tuple(zip(sources, buckets, outs))
    q[...] = jnp.zeros_like(q)

    def listed(src, c):
        return src[MESH_NODES:LISTED, :].astype(F32)[8 * c : 8 * (c + 1), :]

    def geometry_part(d):
        return mm(jnp.concatenate([d, d], axis=1).astype(BF), w_geom[...])

    for i, (src, bucket, _) in enumerate(lists):
        for c in range(CHUNKS):
            row = i * CHUNKS + c
            code = listed(src, c)[0:1, :]
            wanted = float(bucket + 1)
            if bucket < 3 or bucket > 5:
                wanted = jnp.where(band == (7 if bucket < 3 else 0), -1.0, wanted)
            masks[row : row + 1, :] = jnp.where(code == wanted, 1.0, 0.0)
    n = masks.shape[0]
    mask = masks[...]
    before = lax.broadcasted_iota(I32, (CHUNK, CHUNK), 0) < lax.broadcasted_iota(I32, (CHUNK, CHUNK), 1)
    inside = mm(mask.astype(BF), jnp.where(before, 1.0, 0.0).astype(BF))
    mine = lax.broadcasted_iota(I32, (n, n), 0)
    other = lax.broadcasted_iota(I32, (n, n), 1)
    same = mine // CHUNKS == other // CHUNKS
    earlier = jnp.where((other < mine) & same, 1.0, 0.0).astype(BF)
    carried = mm(earlier, mask.astype(BF)).sum(axis=1, keepdims=True)
    ranks[...] = jnp.where(mask > 0.5, inside + carried, -1.0).astype(I32)

    slot = lax.broadcasted_iota(I32, (NEAR_SLOTS, CHUNK), 0)
    for i, (src, _, _) in enumerate(lists):
        d = jnp.zeros((NEAR_SLOTS, 8), F32)
        for c in range(CHUNKS):
            row = i * CHUNKS + c
            d += mm_nt(jnp.where(slot == ranks[row : row + 1, :], 1.0, 0.0).astype(BF), listed(src, c).astype(BF))
        edges[NEAR_SLOTS * i : NEAR_SLOTS * (i + 1), :] = d
    received = mm(jnp.concatenate([src[0:MESH_NODES, :] for src in sources], axis=0), w_recv[...]).astype(BF)
    d = edges[...]
    s = (d[:, 1:2] * 256.0 + d[:, 2:3]).astype(I32)
    pre = mm(one_hot(s, GRID_NODES), send[...]) + geometry_part(d)
    r = jnp.where(d[:, 0:1] > 0.5, d[:, 3:4], -1.0).astype(I32)
    for i, bucket in enumerate(buckets):
        part = slice(NEAR_SLOTS * i, NEAR_SLOTS * (i + 1))
        rows = slice(MESH_NODES * bucket, MESH_NODES * (bucket + 1))
        mine = received[MESH_NODES * i : MESH_NODES * (i + 1), :]
        q[rows, :] = mine
        pick = one_hot(r[part, :], MESH_NODES)
        sums[rows, :] = mm_t(pick, silu(pre[part, :] + mm(pick, mine)).astype(BF))

    count = mm(jnp.where(same, 1.0, 0.0).astype(BF), mask.astype(BF)).sum(axis=1, keepdims=True)
    over = jnp.maximum(count - NEAR_SLOTS, 0.0)
    total = lax.shift_right_logical(jnp.sum(over).astype(I32), 2)

    @pl.when(total > 0)
    def _():
        across = lax.broadcasted_iota(I32, (n, 1), 0) // CHUNKS
        base = jnp.zeros((n, 1), F32)
        for i in range(len(lists) - 1):
            base += jnp.where(across > i, over[i * CHUNKS : i * CHUNKS + 1, :], 0.0)
        rank = ranks[...]
        ranks[...] = jnp.where(rank >= NEAR_SLOTS, rank - NEAR_SLOTS + base.astype(I32), -1)

        @pl.loop(0, lax.shift_right_logical(total + 127, 7))
        def _(k):
            late = lax.broadcasted_iota(I32, (128, CHUNK), 0) + k * 128
            d = jnp.zeros((128, 8), F32)
            for i, (src, _, _) in enumerate(lists):
                for c in range(CHUNKS):
                    row = i * CHUNKS + c
                    d += mm_nt(jnp.where(late == ranks[row : row + 1, :], 1.0, 0.0).astype(BF), listed(src, c).astype(BF))
            s = (d[:, 1:2] * 256.0 + d[:, 2:3]).astype(I32)
            code = d[:, 0:1]
            r = jnp.where(code > 0.5, (code - 1.0) * float(MESH_NODES) + d[:, 3:4], -1.0).astype(I32)
            pick = one_hot(r, 9 * MESH_NODES)
            pre = mm(one_hot(s, GRID_NODES), send[...]) + mm(pick, q[...]) + geometry_part(d)
            sums[...] += mm_t(pick, silu(pre).astype(BF))

    for _, bucket, dst in lists:
        dst[...] = sums[MESH_NODES * bucket : MESH_NODES * (bucket + 1), :].astype(BF)


def corner_body(a, b, c, d, left, right):
    left[0] = a[...]
    left[1] = b[...]
    right[0] = c[...]
    right[1] = d[...]


def side_sum_body(place, above, below, from_left, from_right, order, first, second):
    odd = odd_band(place)
    for k, middle, when_odd, when_even in ((0, above, first, second), (1, below, second, first)):
        total = (middle[...].astype(F32) + from_left[k].astype(F32) + from_right[k].astype(F32)).astype(BF)

        @pl.when(odd)
        def _(total=total, out=when_odd):
            out[...] = total

        @pl.when(jnp.logical_not(odd))
        def _(total=total, out=when_even):
            out[...] = total


def join_body(parts, out):
    n = parts[0].shape[0]
    for k, part in enumerate(parts):
        out[n * k : n * (k + 1), :] = part[...]


def odd_band(place):
    return (lax.shift_right_logical(place[0, 4], 4) & 1) == 1


def pair_body(place, first, second, order, out):
    odd = odd_band(place)

    @pl.when(odd)
    def _():
        out[0] = first[...]
        out[1] = second[...]

    @pl.when(jnp.logical_not(odd))
    def _():
        out[0] = second[...]
        out[1] = first[...]


def partner_body(own, partner, low, both, order, out, onward):
    n = COARSE_DEV
    onward[...] = partner[...]
    for k, part in enumerate((own[...], partner[0:n, :], low[...], both[...])):
        out[n * k : n * (k + 1), :] = part


def bands_body(place, own, partner, below, above, a, b, c, d, order, out, triple):
    join_body((a, b, c, d), out)
    triple[1] = own[...]
    odd = place[0, 2] >= 2

    @pl.when(odd)
    def _():
        triple[0] = partner[...]
        triple[2] = above[...]

    @pl.when(jnp.logical_not(odd))
    def _():
        triple[0] = below[...]
        triple[2] = partner[...]


def node_rows(v, hidden_total, first_node, folded, second):
    u = silu(mm(v, first_node) + mm(hidden_total.astype(BF), folded)).astype(BF)
    return (v.astype(F32) + mm(u, second)).astype(BF)


def node_body(
    own, from_left, from_right, up, down, state, folded, first_node, second, w_send, w_recv, order,
    mesh_one, send, recv, coarse,
):
    total = own[...] + from_left[...].astype(F32) + from_right[...].astype(F32)
    total = total + up[...].astype(F32) + down[...].astype(F32)
    one = node_rows(state[...], total, first_node[...], folded[...], second[...])
    mesh_one[...] = one
    sent = mm(one, w_send[...]).astype(BF)
    send[...] = sent
    coarse[...] = sent[0:COARSE_DEV, :]
    recv[...] = mm(one, w_recv[...]).astype(BF)


def fine_body(edges, left, own, right, recv, w_geom, order, order_too, out, rows):
    parts = (left[1], own[1], right[1], own[0], own[2], left[0], left[2], right[0], right[2])
    for k, part in enumerate(parts):
        rows[MESH_NODES * k : MESH_NODES * (k + 1), :] = part
    q = recv[...].astype(F32)
    total = jnp.zeros((MESH_NODES, WIDTH), F32)
    for t in range(MESH_DEGREE):
        d = edges[t]
        spread = one_hot(d[:, 0:1].astype(I32), 9 * MESH_NODES)
        pre = q + mm(spread, rows[...]) + mm(d.astype(BF), w_geom[...])
        total += silu(pre)
    out[...] = total


def coarse_prep_body(place, own, following, far, out, count, row):
    z, y, x, core, tile = (place[0, k] for k in range(5))
    n = COARSE_EDGES
    lists = (own[...], following[...], far[...])
    for k, edges in enumerate(lists):
        owner = edges.astype(F32)[2:3, :].astype(I32)
        row[k : k + 1, :] = jnp.where(owner == tile, 1.0, 0.0)
    row[3:8, :] = jnp.zeros((5, n), F32)
    mask = row[...]
    before = lax.broadcasted_iota(I32, (n, n), 0) < lax.broadcasted_iota(I32, (n, n), 1)
    inside = mm(mask.astype(BF), jnp.where(before, 1.0, 0.0).astype(BF))
    earlier = lax.broadcasted_iota(I32, (8, 8), 1) < lax.broadcasted_iota(I32, (8, 8), 0)
    carried = mm(jnp.where(earlier, 1.0, 0.0).astype(BF), mask.astype(BF)).sum(axis=1, keepdims=True)
    rank = jnp.where(mask > 0.5, inside + carried, -1.0).astype(I32)
    slot = lax.broadcasted_iota(I32, (3 * n, n), 0)
    d = jnp.zeros((3 * n, 16), F32)
    for k, edges in enumerate(lists):
        d += mm_nt(jnp.where(slot == rank[k : k + 1, :], 1.0, 0.0).astype(BF), edges)
    s = (d[:, 0:1] * 256.0 + d[:, 1:2]).astype(I32)
    t = lax.shift_right_logical(s, 4)
    lat = lax.shift_right_logical(t, 4)
    lon = t & 15
    gz = (z - lax.shift_right_logical(lat, 1)) & 3
    gy = (y - lax.shift_right_logical(lon, 2)) & 3
    g_high = (lax.shift_right_logical(x, 1) + lat) & 1
    g_low = (x + lax.shift_right_logical(lon, 1)) & 1
    gc = (core + lon) & 1
    spot = ((((gc * 4 + gz) * 4 + gy) * 2 + g_low) * 2 + g_high) * 16 + (s & 15)
    total = jnp.sum(mask).astype(I32)
    used = lax.broadcasted_iota(I32, (3 * n, 1), 0) < total
    r = jnp.where(used, d[:, 3:4], -1.0)
    lane = lax.broadcasted_iota(I32, (3 * n, 16), 1)
    out[...] = jnp.where(lane == 0, spot.astype(F32), jnp.where(lane == 1, r, d))
    count[0, 0] = total


def mesh_body(
    count, fine, edges, a0, a1, a2, a3, b0, b1, b2, b3, recv, mesh_one, w_geom, folded, first_node, second, w_send,
    send, rows, total,
):
    parts = (a0, a1, a2, a3, b0, b1, b2, b3)
    n = a0.shape[0]
    for k, part in enumerate(parts):
        rows[n * k : n * (k + 1), :] = part[...]
    q = recv[0:COARSE_DEV, :]

    def hidden_sum(d):
        pick = one_hot(d[:, 1:2].astype(I32), MESH_NODES)
        pre = mm(one_hot(d[:, 0:1].astype(I32), len(parts) * n), rows[...])
        pre += mm(pick[:, 0:COARSE_DEV], q) + mm(d.astype(BF), w_geom[...])
        return mm_t(pick, silu(pre).astype(BF))

    total[...] = fine[...] + hidden_sum(edges[0:COARSE_SLOTS, :])

    @pl.loop(COARSE_SLOTS // 64, lax.shift_right_logical(count[0, 0] + 63, 6))
    def _(k):
        total[...] += hidden_sum(edges[pl.ds(pl.multiple_of(64 * k, 64), 64), :])

    two = node_rows(mesh_one[...], total[...], first_node[...], folded[...], second[...])
    send[...] = mm(two, w_send[...]).astype(BF)


def decode_early_body(edges, left, own, right, pair, recv, w_geom, out, rows):
    for k, part in enumerate((left, own, right, pair.at[0], pair.at[1])):
        rows[MESH_NODES * k : MESH_NODES * (k + 1), :] = part[...]
    n = 5 * MESH_NODES

    @pl.loop(0, 4)
    def _(b):
        span = pl.ds(pl.multiple_of(256 * b, 256), 256)
        q = recv[span, :].astype(F32)
        for t in range(GRID_DEGREE):
            d = edges[t, span, :]
            spread = one_hot(d[:, 0:1].astype(I32), n)
            out[t, span, :] = q + mm(spread, rows[0:n, :]) + mm(d.astype(BF), w_geom[...])


def decode_body(edges, early, left_pair, right_pair, base, folded, head, out, rows, totals):
    for k, part in enumerate((left_pair.at[0], left_pair.at[1], right_pair.at[0], right_pair.at[1])):
        rows[MESH_NODES * k : MESH_NODES * (k + 1), :] = part[...]
    @pl.loop(0, 4)
    def _(b):
        span = pl.ds(pl.multiple_of(256 * b, 256), 256)
        total = jnp.zeros((256, WIDTH), F32)
        for t in range(GRID_DEGREE):
            spot = edges[t, span, :][:, 0:1].astype(I32) - 5 * MESH_NODES
            total += silu(early[t, span, :] + mm(one_hot(spot, 4 * MESH_NODES), rows[...]))
        totals[span, :] = total.astype(BF)

    @pl.loop(0, 2)
    def _(b):
        span = pl.ds(pl.multiple_of(512 * b, 512), 512)
        hidden = silu(base[span, :] + mm(totals[span, :], folded[...])).astype(BF)
        out[:, span] = mm_nt(head[...], hidden).astype(BF)


def shift(value, axis, step, periodic):
    n = lax.axis_size(axis)
    pairs = [(i, (i + step) % n) for i in range(n) if periodic or 0 <= i + step < n]
    return lax.ppermute(value, axis, pairs)


def swap_bands(first, second, wrap=False):
    later = [(i, (i + 1) % 8) for i in (1, 3, 5, 7) if wrap or i < 7]
    later += [(target, source) for source, target in later]
    second = lax.ppermute(second, "lat", later)
    return lax.ppermute(first, "lat", [(i, i ^ 1) for i in range(8)]), second


def first_stage(value, wrap=False):
    first, second = swap_bands(value, value, wrap)
    return first, second, shift(value, "lon", 1, True), shift(value, "lon", -1, True)


def second_stage(pair):
    return shift(pair, "lon", 1, True), shift(pair, "lon", -1, True)


def along_z(s):
    return [(i, ((i // 2 + s) % 4) * 2 + i % 2) for i in range(8)]


def along_y(s):
    return [(i, ((i // 4 + s) % 4) * 4 + i % 4) for i in range(16)]


def per_device(
    grid_inputs,
    mesh_state,
    embed_in,
    embed_out,
    edge_square,
    edge_geom_weight,
    node_first,
    node_second,
    head,
    g2m_senders,
    g2m_receivers,
    g2m_counts,
    g2m_geom,
    mesh_senders,
    mesh_geom,
    coarse_senders,
    coarse_receivers,
    coarse_geom,
    m2g_senders,
    m2g_geom,
):
    mesh_rows = (MESH_NODES, WIDTH)
    grid_rows = (GRID_NODES, WIDTH)
    pair_rows = (2,) + mesh_rows
    grid_flops = 2 * GRID_NODES * WIDTH * WIDTH
    mesh_flops = grid_flops // 8
    both = ("lat", "lon")
    tiles = lax.axis_size(both)
    lat, lon = lax.axis_index("lat"), lax.axis_index("lon")
    place = jnp.stack([lat // 2, lon // 4, (lat % 2) * 2 + (lon // 2) % 2, lon % 2, lat * LON + lon])[None]
    place = place.astype(I32)

    pack_args = (
        g2m_senders, g2m_receivers, g2m_geom, mesh_state, coarse_senders, coarse_receivers, coarse_geom
    )

    def part_of(array):
        n = array.ndim - 2
        return Load((0,) if n == 1 else (0, 0), array.shape[1:] if n == 1 else array.shape[2:])

    payload, own_list, coarse_list, geom = kernel_call(
        pack_body,
        (
            shaped((PAYLOAD, WIDTH), BF), shaped((16 * CHUNKS, WIDTH), BF), shaped((16, COARSE_EDGES), BF),
            shaped((4, 16, WIDTH), BF),
        ),
        [SMEM] + [part_of(a) for a in pack_args] + [Load((), edge_geom_weight.shape)],
        (g2m_counts,) + pack_args + (edge_geom_weight,),
        [pltpu.VMEM((16, CHUNK), F32), pltpu.VMEM((8 * CHUNKS, CHUNK), F32)],
        name="pack",
    )
    first, second, near_left, near_right = first_stage(payload, True)
    turned_inputs = jnp.swapaxes(grid_inputs, 2, 3)
    latent, w_send = kernel_call(
        embed_body,
        (shaped(grid_rows, BF), shaped((WIDTH, WIDTH), BF)),
        [part_of(turned_inputs), Load((), embed_in.shape), Load((), embed_out.shape), HBM],
        (turned_inputs, embed_in, embed_out, edge_square),
        [pltpu.SemaphoreType.DMA((1,))],
        flops=2 * grid_flops,
        moved=4 << 20,
        name="embed",
    )
    grid_send = kernel_call(
        send_body,
        shaped(grid_rows, BF),
        [V, V, ANY, ANY],
        (latent, w_send, near_left, near_right),
        flops=grid_flops,
        moved=3 << 20,
        name="send",
    )

    def geom_of(k):
        return View(k)

    own_specs = [part_of(mesh_state), V, V, square(0, 1), geom_of(0)]
    own_args = (mesh_state, own_list, grid_send, edge_square, geom)

    def paired(first, second, order):
        shape = (2,) + first.shape
        return kernel_call(
            pair_body, shaped(shape, BF), [SMEM, V, V, ANY], (place, first, second, order), name="pair"
        )

    own_first, list_rest = kernel_call(
        functools.partial(self_body, (0, 1)),
        (shaped(mesh_rows, F32), shaped((32, WIDTH), BF)),
        own_specs,
        own_args,
        flops=2 * grid_flops,
        moved=3 << 20,
        name="own_first",
    )
    near_middle = paired(first, second, own_first)
    near_left_pair, near_right_pair = second_stage(near_middle)
    own_sum = kernel_call(
        functools.partial(self_body, (0, 1)),
        shaped(mesh_rows, F32),
        own_specs + [V],
        (mesh_state, list_rest, grid_send, edge_square, geom, own_first),
        flops=2 * grid_flops,
        moved=3 << 20,
        name="own_last",
    )
    near_scratch = [
        pltpu.VMEM((4 * CHUNKS, CHUNK), F32),
        pltpu.VMEM((4 * CHUNKS, CHUNK), I32),
        pltpu.VMEM((9 * MESH_NODES, WIDTH), BF),
        pltpu.VMEM((4 * NEAR_SLOTS, 8), F32),
        pltpu.VMEM((9 * MESH_NODES, WIDTH), F32),
    ]
    near_weights = [V, square(0, 1), geom_of(3)]
    to_left, to_right, to_above, to_below, right_list = kernel_call(
        functools.partial(near_body, (5, 3, 7, 1)),
        (shaped(mesh_rows, BF),) * 4 + (shaped((16, COARSE_EDGES), BF),),
        [SMEM, V, V, View(0), View(1)] + near_weights,
        (place, near_left, near_right, near_middle, near_middle, grid_send, edge_square, geom),
        near_scratch,
        flops=2 * grid_flops,
        moved=5 << 20,
        name="beside",
    )
    *to_corners, coarse_next = kernel_call(
        functools.partial(near_body, (8, 2, 6, 0)),
        (shaped(mesh_rows, BF),) * 4 + (shaped((16, COARSE_EDGES), BF),),
        [SMEM, View(0), View(1), View(0), View(1), V, ANY, ANY] + near_weights,
        (
            place, near_left_pair, near_left_pair, near_right_pair, near_right_pair, right_list, own_sum, to_left,
            grid_send, edge_square, geom,
        ),
        near_scratch,
        flops=2 * grid_flops,
        moved=5 << 20,
        name="corners",
    )
    to_left_pair, to_right_pair = kernel_call(
        corner_body, (shaped(pair_rows, BF),) * 2, [V] * 4, tuple(to_corners), name="corner_pairs"
    )
    pair_left = shift(to_right_pair, "lon", 1, True)
    pair_right = shift(to_left_pair, "lon", -1, True)
    prep_args = (mesh_senders, mesh_geom, m2g_senders, m2g_geom)
    stored = {"square": edge_square, "first": node_first, "second": node_second}
    m_edges, d_edges, to_left, to_right, *kept = kernel_call(
        prep_body,
        (
            shaped((MESH_DEGREE, MESH_NODES, 16), F32),
            shaped((GRID_DEGREE, GRID_NODES, 16), F32),
            shaped(mesh_rows, BF),
            shaped(mesh_rows, BF),
        ) + (shaped((WIDTH, WIDTH), BF),) * len(KEPT),
        [part_of(a) for a in prep_args] + [V, V, ANY] + [HBM] * len(KEPT),
        prep_args + (to_left, to_right, to_left_pair) + tuple(stored[name] for name, _ in KEPT),
        [pltpu.VMEM((16, 3072), F32), pltpu.VMEM((3072, 16), F32), pltpu.SemaphoreType.DMA((len(KEPT),))],
        flops=grid_flops,
        name="prep",
    )
    to_first, to_second = kernel_call(
        side_sum_body,
        (shaped(mesh_rows, BF),) * 2,
        [SMEM, V, V, V, V, ANY],
        (place, to_above, to_below, pair_left, pair_right, m_edges),
        name="sides",
    )
    up, down = swap_bands(to_first, to_second)
    folded = kernel_call(
        fold_body,
        (shaped((WIDTH, WIDTH), BF),) * 3,
        [part for k in range(3) for part in (square(k, 2), first_half(k, 1))] + [ANY],
        (edge_square, node_first) * 3 + (to_first,),
        flops=3 * grid_flops // 2,
        moved=4 << 20,
        name="fold",
    )
    from_left = shift(to_right, "lon", 1, True)
    from_right = shift(to_left, "lon", -1, True)
    far_list = lax.ppermute(coarse_list, both, [(t, (t + tiles // 2) % tiles) for t in range(tiles)])
    mesh_one, proc_send, proc_recv, coarse_own = kernel_call(
        node_body,
        (shaped(mesh_rows, BF),) * 3 + (shaped((COARSE_DEV, WIDTH), BF),),
        [V] * 5 + [part_of(mesh_state)] + [V] * 5 + [ANY],
        (own_sum, from_left, from_right, up, down, mesh_state, folded[0], *kept[0:4], far_list),
        flops=7 * mesh_flops,
        moved=4 << 20,
        name="node",
    )
    grid_recv, grid_base = kernel_call(
        grid_body,
        (shaped(grid_rows, BF), shaped(grid_rows, F32)),
        [V, square(2, 1), first_half(2, 0), ANY],
        (latent, edge_square, node_first, proc_send),
        flops=2 * grid_flops,
        moved=5 << 20,
        name="grid",
    )
    def half(t):
        return (t // LON ^ 1) * LON + (t % LON)

    partner = lax.ppermute(proc_send, "lat", [(i, i ^ 1) for i in range(8)])
    low = lax.ppermute(coarse_own, "lon", [(i, i ^ 2) for i in range(LON)])
    cross = lax.ppermute(coarse_own, both, [(t, half(t) ^ 2) for t in range(tiles)])
    beside, onward = kernel_call(
        partner_body,
        (shaped((4 * COARSE_DEV, WIDTH), BF), shaped(mesh_rows, BF)),
        [V, V, V, V, ANY],
        (coarse_own, partner, low, cross, grid_recv),
        name="partner",
    )
    edge_total = 3 * COARSE_EDGES
    c_edges, c_count = kernel_call(
        coarse_prep_body,
        (shaped((edge_total, 16), F32), shaped((1, 1), I32)),
        [SMEM, V, V, V],
        (place, coarse_list, coarse_next, far_list),
        [pltpu.VMEM((8, COARSE_EDGES), F32)],
        flops=mesh_flops,
        name="coarse_edges",
        out_specs=(V, SMEM),
    )
    quarter = [beside] + [lax.ppermute(beside, "lon", along_y(s)) for s in (1, 2, 3)]
    below = lax.ppermute(onward, "lat", along_z(1))
    above = lax.ppermute(onward, "lat", along_z(3))
    rows, triple = kernel_call(
        bands_body,
        (shaped((16 * COARSE_DEV, WIDTH), BF), shaped((3,) + mesh_rows, BF)),
        [SMEM] + [V] * 8 + [ANY],
        (place, proc_send, onward, below, above, *quarter, c_edges),
        name="bands",
    )
    left, right = second_stage(triple)
    quarter = [rows] + [lax.ppermute(rows, "lat", along_z(s)) for s in (1, 2, 3)]
    swapped = [lax.ppermute(part, "lon", [(i, i ^ 1) for i in range(LON)]) for part in quarter]
    fine = kernel_call(
        fine_body,
        shaped(mesh_rows, F32),
        [V] * 5 + [geom_of(1), ANY, ANY],
        (m_edges, left, triple, right, proc_recv, geom, quarter[1], c_edges),
        [pltpu.VMEM((9 * MESH_NODES, WIDTH), BF)],
        flops=2 * grid_flops,
        moved=3 << 20,
        name="fine",
    )
    dec_send = kernel_call(
        mesh_body,
        shaped(mesh_rows, BF),
        [SMEM] + [V] * 12 + [geom_of(1)] + [V] * 4,
        (c_count, fine, c_edges, *quarter, *swapped, proc_recv, mesh_one, geom, folded[1], *kept[4:7]),
        [pltpu.VMEM((128 * COARSE_DEV, WIDTH), BF), pltpu.VMEM(mesh_rows, F32)],
        flops=4 * grid_flops,
        moved=6 << 20,
        name="mesh",
    )
    first, second, left, right = first_stage(dec_send)
    pair = paired(first, second, dec_send)
    left_pair, right_pair = second_stage(pair)
    early = kernel_call(
        decode_early_body,
        shaped((GRID_DEGREE,) + grid_rows, F32),
        [V, V, V, V, V, V, geom_of(2)],
        (d_edges, left, dec_send, right, pair, grid_recv, geom),
        [pltpu.VMEM((5 * MESH_NODES, WIDTH), BF)],
        flops=4 * grid_flops,
        moved=8 << 20,
        name="early",
    )
    outputs = kernel_call(
        decode_body,
        shaped((head.shape[1], GRID_NODES), BF),
        [V] * 7,
        (d_edges, early, left_pair, right_pair, grid_base, folded[2], head.T),
        [pltpu.VMEM((4 * MESH_NODES, WIDTH), BF), pltpu.VMEM(grid_rows, BF)],
        flops=5 * grid_flops,
        moved=8 << 20,
        name="decode",
    )
    return outputs.T[None, None]


def solution(mesh):
    return jax.shard_map(
        per_device,
        mesh=mesh,
        in_specs=(
            P("lat", "lon", None, None),
            P("lat", "lon", None, None),
            P(),
            P(),
            P(),
            P(),
            P(),
            P(),
            P(),
            P("lat", "lon", None),
            P("lat", "lon", None),
            P("lat", "lon"),
            P("lat", "lon", None, None),
            P("lat", "lon", None),
            P("lat", "lon", None, None),
            P("lat", "lon", None),
            P("lat", "lon", None),
            P("lat", "lon", None, None),
            P("lat", "lon", None),
            P("lat", "lon", None, None),
        ),
        out_specs=P("lat", "lon", None, None),
        check_vma=False,
    )
```

profile of v0, /device:TPU:4, one launch (start us, length us, event | category | flops | bytes accessed | tf_op | source)
XLA Modules:
  0.0 128.0 jit_solution(16207526013636319527)
XLA Ops:
  1.8 3.8 %collective-permute-start.1 = (bf16[176,512]{1,0:T(8,128)(2,1)S(1)}, bf16[176,512]{1,0:T(8,128)(2,1)S(1)}, u32[]{:S(2)}, u32[]{:S(2)}) collective-permute-start(bf16[176,512]{1,0:T(8,128)(2,1)S(1)} %get-tuple-element.53), channel_id=1, source_target_pairs={{0,15},{1,0},{2,1},{3,2},{4,3},{5,4},{6,5},{7,6},{8,7},{9,8},{10,9... | collective-permute-start | bytes 540680 | tf_op jit(solution)/shard_map/ppermute | solution.py:589
  6.0 4.5 %collective-permute-start.3 = (bf16[176,512]{1,0:T(8,128)(2,1)S(1)}, bf16[176,512]{1,0:T(8,128)(2,1)S(1)}, u32[]{:S(2)}, u32[]{:S(2)}) collective-permute-start(bf16[176,512]{1,0:T(8,128)(2,1)S(1)} %get-tuple-element.53), channel_id=1, source_target_pairs={{16,32},{48,64},{80,96},{112,0},{32,16},{64,48},{96,80},{0,112},{1... | collective-permute-start | bytes 540680 | tf_op jit(solution)/shard_map/ppermute | solution.py:595
  10.5 3.9 %embed.1 = (bf16[1024,512]{1,0:T(8,128)(2,1)S(1)}, bf16[512,512]{1,0:T(8,128)(2,1)S(1)}) custom-call(bf16[1,1,474,1024]{3,2,1,0:T(8,128)(2,1)} %bitcast.19, bf16[474,512]{1,0:T(8,128)(2,1)} %refs_1_.6, bf16[512,512]{1,0:T(8,128)(2,1)} %refs_2_.6, bf16[3,3,512,512]{3,2,1,0:T(8,128)(2,1)} %refs_1_.9), custom_call_target="tpu_custom_call" | custom-call | flops 1073741824 | bytes 4194304 | tf_op jit(solution)/shard_map/embed/pallas_call | solution.py:135
  15.5 2.9 %own_first.1 = (f32[128,512]{1,0:T(8,128)S(1)}, bf16[32,512]{1,0:T(8,128)(2,1)S(1)}) custom-call(bf16[1,1,128,512]{3,2,1,0:T(8,128)(2,1)} %refs_5_.5, bf16[64,512]{1,0:T(8,128)(2,1)S(1)} %get-tuple-element.54.refs_1_, bf16[1024,512]{1,0:T(8,128)(2,1)S(1)} %send.1.refs_2_.refs_5_.refs_8_, bf16[3,3,512,512]{3,2,1,0:T(8,128)(2,1)} %refs_1_.9, ...), custom_call_target="tpu_custom_call" | custom-call | flops 1073741824 | bytes 3145728 | tf_op jit(solution)/shard_map/own_first/pallas_call | solution.py:135
  19.1 3.8 %collective-permute-start.5 = (bf16[2,176,512]{2,1,0:T(8,128)(2,1)S(1)}, bf16[2,176,512]{2,1,0:T(8,128)(2,1)S(1)}, u32[]{:S(2)}, u32[]{:S(2)}) collective-permute-start(bf16[2,176,512]{2,1,0:T(8,128)(2,1)S(1)} %pair.2.refs_3_.refs_4_), channel_id=1, source_target_pairs={{0,15},{1,0},{2,1},{3,2},{4,3},{5,4},{6,5},{7,6},{8,7},{9,8},{10,9... | collective-permute-start | bytes 1081352 | tf_op jit(solution)/shard_map/ppermute | solution.py:589
  22.9 3.0 %own_last.1.refs_6_.refs_0_ = f32[128,512]{1,0:T(8,128)S(1)} custom-call(bf16[1,1,128,512]{3,2,1,0:T(8,128)(2,1)} %refs_5_.5, bf16[32,512]{1,0:T(8,128)(2,1)S(1)} %get-tuple-element.62.refs_1_, bf16[1024,512]{1,0:T(8,128)(2,1)S(1)} %send.1.refs_2_.refs_5_.refs_8_, bf16[3,3,512,512]{3,2,1,0:T(8,128)(2,1)} %refs_1_.9, ...), custom_call_target="tpu_custom_call" | custom-call | flops 1073741824 | bytes 3145728 | tf_op jit(solution)/shard_map/own_last/pallas_call | solution.py:135
  25.9 4.4 %beside.1 = (bf16[128,512]{1,0:T(8,128)(2,1)S(1)}, bf16[128,512]{1,0:T(8,128)(2,1)S(1)}, bf16[128,512]{1,0:T(8,128)(2,1)S(1)}, bf16[128,512]{1,0:T(8,128)(2,1)S(1)}, bf16[16,256]{1,0:T(8,128)(2,1)S(1)}) custom-call(s32[1,5]{1,0:T(1,128)S(1)} %bitcast.13, bf16[176,512]{1,0:T(8,128)(2,1)S(1)} %collective-permute-done.refs_2_.refs_1_, ...), custom_call_target="tpu_custom_call" | custom-call | flops 1073741824 | bytes 5242880 | tf_op jit(solution)/shard_map/beside/pallas_call | solution.py:135
  31.0 4.2 %corners.1 = (bf16[128,512]{1,0:T(8,128)(2,1)S(1)}, bf16[128,512]{1,0:T(8,128)(2,1)S(1)}, bf16[128,512]{1,0:T(8,128)(2,1)S(1)}, bf16[128,512]{1,0:T(8,128)(2,1)S(1)}, bf16[16,256]{1,0:T(8,128)(2,1)S(1)}) custom-call(s32[1,5]{1,0:T(1,128)S(1)} %bitcast.14, bf16[2,176,512]{2,1,0:T(8,128)(2,1)S(1)} %collective-permute-done.4.refs_1_.refs_2_, ...), custom_call_target="tpu_custom_call" | custom-call | flops 1073741824 | bytes 5242880 | tf_op jit(solution)/shard_map/corners/pallas_call | solution.py:135
  35.3 1.8 %collective-permute-start.10 = (bf16[2,128,512]{2,1,0:T(8,128)(2,1)S(1)}, bf16[2,128,512]{2,1,0:T(8,128)(2,1)S(1)}, u32[]{:S(2)}, u32[]{:S(2)}) collective-permute-start(bf16[2,128,512]{2,1,0:T(8,128)(2,1)S(1)} %get-tuple-element.67.refs_6_), channel_id=1, source_target_pairs={{0,15},{1,0},{2,1},{3,2},{4,3},{5,4},{6,5},{7,6},{8,7},{9,8},{10,9... | collective-permute-start | bytes 786440 | tf_op jit(solution)/shard_map/ppermute | solution.py:589
  37.0 2.5 %prep.1 = (f32[6,128,16]{2,1,0:T(8,128)S(1)}, f32[3,1024,16]{2,1,0:T(8,128)S(1)}, bf16[128,512]{1,0:T(8,128)(2,1)S(1)}, bf16[128,512]{1,0:T(8,128)(2,1)S(1)}, bf...) custom-call(s32[1,1,768]{2,1,0:T(1,128)} %refs_0_.7, ...), custom_call_target="tpu_custom_call" | custom-call | flops 536870912 | tf_op jit(solution)/shard_map/prep/pallas_call | solution.py:135
  39.7 3.9 %collective-permute-start.8 = (bf16[128,512]{1,0:T(8,128)(2,1)S(1)}, bf16[128,512]{1,0:T(8,128)(2,1)S(1)}, u32[]{:S(2)}, u32[]{:S(2)}) collective-permute-start(bf16[128,512]{1,0:T(8,128)(2,1)S(1)} %get-tuple-element.74), channel_id=1, source_target_pairs={{0,15},{1,0},{2,1},{3,2},{4,3},{5,4},{6,5},{7,6},{8,7},{9,8},{10,9... | collective-permute-start | bytes 393224 | tf_op jit(solution)/shard_map/ppermute | solution.py:589
  45.6 4.3 %collective-permute-start.11 = (bf16[128,512]{1,0:T(8,128)(2,1)S(1)}, bf16[128,512]{1,0:T(8,128)(2,1)S(1)}, u32[]{:S(2)}, u32[]{:S(2)}) collective-permute-start(bf16[128,512]{1,0:T(8,128)(2,1)S(1)} %get-tuple-element.78.refs_6_), channel_id=1, source_target_pairs={{0,16},{16,0},{32,48},{48,32},{64,80},{80,64},{96,112},{112,96},{1... | collective-permute-start | bytes 393224 | tf_op jit(solution)/shard_map/ppermute | solution.py:596
  50.0 2.5 %collective-permute-start.12 = (bf16[128,512]{1,0:T(8,128)(2,1)S(1)}, bf16[128,512]{1,0:T(8,128)(2,1)S(1)}, u32[]{:S(2)}, u32[]{:S(2)}) collective-permute-start(bf16[128,512]{1,0:T(8,128)(2,1)S(1)} %get-tuple-element.79), channel_id=1, source_target_pairs={{16,32},{48,64},{80,96},{32,16},{64,48},{96,80},{17,33},{49,65},{8... | collective-permute-start | bytes 393224 | tf_op jit(solution)/shard_map/ppermute | solution.py:595
  53.4 2.6 %fold.1 = (bf16[512,512]{1,0:T(8,128)(2,1)S(1)}, bf16[512,512]{1,0:T(8,128)(2,1)S(1)}, bf16[512,512]{1,0:T(8,128)(2,1)S(1)}) custom-call(bf16[3,3,512,512]{3,2,1,0:T(8,128)(2,1)} %refs_1_.9, bf16[3,1024,512]{2,1,0:T(8,128)(2,1)} %refs_2_.9, bf16[3,3,512,512]{3,2,1,0:T(8,128)(2,1)} %refs_1_.9, bf16[3,1024,512]{2,1,0:T(8,128)(2,1)} %refs_2_.9, ...), custom_call_target="tpu_custom_call" | custom-call | flops 805306368 | bytes 4194304 | tf_op jit(solution)/shard_map/fold/pallas_call | solution.py:135
  59.2 1.7 %node.1 = (bf16[128,512]{1,0:T(8,128)(2,1)S(1)}, bf16[128,512]{1,0:T(8,128)(2,1)S(1)}, bf16[128,512]{1,0:T(8,128)(2,1)S(1)}, bf16[16,512]{1,0:T(8,128)(2,1)S(1)}) custom-call(f32[128,512]{1,0:T(8,128)S(1)} %own_last.1.refs_6_.refs_0_, bf16[128,512]{1,0:T(8,128)(2,1)S(1)} %collective-permute-done.7.refs_1_, ...), custom_call_target="tpu_custom_call" | custom-call | flops 469762048 | bytes 4194304 | tf_op jit(solution)/shard_map/node/pallas_call | solution.py:135
  62.1 3.0 %collective-permute-start.15 = (bf16[16,512]{1,0:T(8,128)(2,1)S(1)}, bf16[16,512]{1,0:T(8,128)(2,1)S(1)}, u32[]{:S(2)}, u32[]{:S(2)}) collective-permute-start(bf16[16,512]{1,0:T(8,128)(2,1)S(1)} %get-tuple-element.86.refs_0_), channel_id=1, source_target_pairs={{0,18},{1,19},{2,16},{3,17},{4,22},{5,23},{6,20},{7,21},{8,26},{9,... | collective-permute-start | bytes 49160 | tf_op jit(solution)/shard_map/ppermute | solution.py:817
  65.1 3.0 %grid.1 = (bf16[1024,512]{1,0:T(8,128)(2,1)S(1)}, f32[1024,512]{1,0:T(8,128)S(1)}) custom-call(bf16[1024,512]{1,0:T(8,128)(2,1)S(1)} %get-tuple-element.55.refs_0_, bf16[3,3,512,512]{3,2,1,0:T(8,128)(2,1)} %refs_1_.9, bf16[3,1024,512]{2,1,0:T(8,128)(2,1)} %refs_2_.9, bf16[128,512]{1,0:T(8,128)(2,1)S(1)} %get-tuple-element.85.refs_3_.refs_1_), custom_call_target="tpu_custom_call" | custom-call | flops 1073741824 | bytes 5242880 | tf_op jit(solution)/shard_map/grid/pallas_call | solution.py:135
  68.3 3.1 %collective-permute-start.17 = (bf16[128,512]{1,0:T(8,128)(2,1)S(1)}, bf16[128,512]{1,0:T(8,128)(2,1)S(1)}, u32[]{:S(2)}, u32[]{:S(2)}) collective-permute-start(bf16[128,512]{1,0:T(8,128)(2,1)S(1)} %get-tuple-element.88.refs_2_), channel_id=1, source_target_pairs={{0,96},{16,112},{32,0},{48,16},{64,32},{80,48},{96,64},{112,80},{1... | collective-permute-start | bytes 393224 | tf_op jit(solution)/shard_map/ppermute | solution.py:838
  72.7 2.1 %collective-permute-start.19 = (bf16[64,512]{1,0:T(8,128)(2,1)S(1)}, bf16[64,512]{1,0:T(8,128)(2,1)S(1)}, u32[]{:S(2)}, u32[]{:S(2)}) collective-permute-start(bf16[64,512]{1,0:T(8,128)(2,1)S(1)} %get-tuple-element.89.refs_5_), channel_id=1, source_target_pairs={{0,8},{1,9},{2,10},{3,11},{4,12},{5,13},{6,14},{7,15},{8,0},{9,1},... | collective-permute-start | bytes 196616 | tf_op jit(solution)/shard_map/ppermute | solution.py:836
  74.8 1.9 %collective-permute-start.20 = (bf16[64,512]{1,0:T(8,128)(2,1)S(1)}, bf16[64,512]{1,0:T(8,128)(2,1)S(1)}, u32[]{:S(2)}, u32[]{:S(2)}) collective-permute-start(bf16[64,512]{1,0:T(8,128)(2,1)S(1)} %get-tuple-element.89.refs_5_), channel_id=1, source_target_pairs={{0,12},{1,13},{2,14},{3,15},{4,0},{5,1},{6,2},{7,3},{8,4},{9,5},{1... | collective-permute-start | bytes 196616 | tf_op jit(solution)/shard_map/ppermute | solution.py:836
  76.7 1.7 %coarse_edges.1 = (f32[768,16]{1,0:T(8,128)S(1)}, s32[1,1]{1,0:T(1,128)}) custom-call(s32[1,5]{1,0:T(1,128)S(1)} %bitcast.16, bf16[16,256]{1,0:T(8,128)(2,1)S(1)} %get-tuple-element.69.refs_1_, bf16[16,256]{1,0:T(8,128)(2,1)S(1)} %get-tuple-element.70.refs_2_, bf16[16,256]{1,0:T(8,128)(2,1)S(1)} %collective-permute-done.6.refs_3_.refs_11_), custom_call_target="tpu_custom_call" | custom-call | flops 67108864 | tf_op jit(solution)/shard_map/coarse_edges/pallas_call | solution.py:135
  81.3 1.8 %collective-permute-start.25 = (bf16[256,512]{1,0:T(8,128)(2,1)S(1)}, bf16[256,512]{1,0:T(8,128)(2,1)S(1)}, u32[]{:S(2)}, u32[]{:S(2)}) collective-permute-start(bf16[256,512]{1,0:T(8,128)(2,1)S(1)} %get-tuple-element.93.refs_3_), channel_id=1, source_target_pairs={{0,96},{16,112},{32,0},{48,16},{64,32},{80,48},{96,64},{112,80},{1... | collective-permute-start | bytes 786440 | tf_op jit(solution)/shard_map/ppermute | solution.py:847
  83.1 3.2 %collective-permute-start.22 = (bf16[3,128,512]{2,1,0:T(8,128)(2,1)S(1)}, bf16[3,128,512]{2,1,0:T(8,128)(2,1)S(1)}, u32[]{:S(2)}, u32[]{:S(2)}) collective-permute-start(bf16[3,128,512]{2,1,0:T(8,128)(2,1)S(1)} %get-tuple-element.91.refs_2_), channel_id=1, source_target_pairs={{0,15},{1,0},{2,1},{3,2},{4,3},{5,4},{6,5},{7,6},{8,7},{9,8},{10,9... | collective-permute-start | bytes 1179656 | tf_op jit(solution)/shard_map/ppermute | solution.py:589
  86.3 8.9 %collective-permute-done.23.refs_6_.refs_4_ = bf16[256,512]{1,0:T(8,128)(2,1)S(1)} collective-permute-done((bf16[256,512]{1,0:T(8,128)(2,1)S(1)}, bf16[256,512]{1,0:T(8,128)(2,1)S(1)}, u32[]{:S(2)}, u32[]{:S(2)}) %collective-permute-start.23) | collective-permute-done | bytes 262176 | tf_op jit(solution)/shard_map/ppermute | solution.py:847
  96.9 1.7 %fine.1.refs_1_ = f32[128,512]{1,0:T(8,128)S(1)} custom-call(f32[6,128,16]{2,1,0:T(8,128)S(1)} %get-tuple-element.72.refs_5_.refs_0_, bf16[3,128,512]{2,1,0:T(8,128)(2,1)S(1)} %collective-permute-done.21.refs_1_, bf16[3,128,512]{2,1,0:T(8,128)(2,1)S(1)} %get-tuple-element.91.refs_2_, bf16[3,128,512]{2,1,0:T(8,128)(2,1)S(1)} %collective-permute-done.22.refs_3_, ...), custom_call_target="tpu_custom_call" | custom-call | flops 1073741824 | bytes 3145728 | tf_op jit(solution)/shard_map/fine/pallas_call | solution.py:135
  98.7 2.5 %mesh.1.refs_3_.refs_2_ = bf16[128,512]{1,0:T(8,128)(2,1)S(1)} custom-call(s32[1,1]{1,0:T(1,128)} %get-tuple-element.71.refs_0_, f32[128,512]{1,0:T(8,128)S(1)} %fine.1.refs_1_, f32[768,16]{1,0:T(8,128)S(1)} %get-tuple-element.90.refs_9_.refs_7_.refs_2_, bf16[256,512]{1,0:T(8,128)(2,1)S(1)} %get-tuple-element.93.refs_3_, ...), custom_call_target="tpu_custom_call" | custom-call | flops 2147483648 | bytes 6291456 | tf_op jit(solution)/shard_map/mesh/pallas_call | solution.py:135
  102.7 3.8 %collective-permute-start.33 = (bf16[128,512]{1,0:T(8,128)(2,1)S(1)}, bf16[128,512]{1,0:T(8,128)(2,1)S(1)}, u32[]{:S(2)}, u32[]{:S(2)}) collective-permute-start(bf16[128,512]{1,0:T(8,128)(2,1)S(1)} %mesh.1.refs_3_.refs_2_), channel_id=1, source_target_pairs={{16,32},{48,64},{80,96},{32,16},{64,48},{96,80},{17,33},{49,65},{8... | collective-permute-start | bytes 393224 | tf_op jit(solution)/shard_map/ppermute | solution.py:595
  106.6 3.8 %collective-permute-start.31 = (bf16[128,512]{1,0:T(8,128)(2,1)S(1)}, bf16[128,512]{1,0:T(8,128)(2,1)S(1)}, u32[]{:S(2)}, u32[]{:S(2)}) collective-permute-start(bf16[128,512]{1,0:T(8,128)(2,1)S(1)} %mesh.1.refs_3_.refs_2_), channel_id=1, source_target_pairs={{0,15},{1,0},{2,1},{3,2},{4,3},{5,4},{6,5},{7,6},{8,7},{9,8},{10,9... | collective-permute-start | bytes 393224 | tf_op jit(solution)/shard_map/ppermute | solution.py:589
  110.4 2.9 %collective-permute-done.33.refs_2_ = bf16[128,512]{1,0:T(8,128)(2,1)S(1)} collective-permute-done((bf16[128,512]{1,0:T(8,128)(2,1)S(1)}, bf16[128,512]{1,0:T(8,128)(2,1)S(1)}, u32[]{:S(2)}, u32[]{:S(2)}) %collective-permute-start.33) | collective-permute-done | bytes 131104 | tf_op jit(solution)/shard_map/ppermute | solution.py:595
  114.0 3.8 %collective-permute-start.35 = (bf16[2,128,512]{2,1,0:T(8,128)(2,1)S(1)}, bf16[2,128,512]{2,1,0:T(8,128)(2,1)S(1)}, u32[]{:S(2)}, u32[]{:S(2)}) collective-permute-start(bf16[2,128,512]{2,1,0:T(8,128)(2,1)S(1)} %pair.3.refs_4_), channel_id=1, source_target_pairs={{0,15},{1,0},{2,1},{3,2},{4,3},{5,4},{6,5},{7,6},{8,7},{9,8},{10,9... | collective-permute-start | bytes 786440 | tf_op jit(solution)/shard_map/ppermute | solution.py:589
  117.9 4.5 %early.1.refs_1_ = f32[3,1024,512]{2,1,0:T(8,128)S(1)} custom-call(f32[3,1024,16]{2,1,0:T(8,128)S(1)} %get-tuple-element.68.refs_0_, bf16[128,512]{1,0:T(8,128)(2,1)S(1)} %collective-permute-done.30.refs_1_, bf16[128,512]{1,0:T(8,128)(2,1)S(1)} %mesh.1.refs_3_.refs_2_, bf16[128,512]{1,0:T(8,128)(2,1)S(1)} %collective-permute-done.31.refs_3_, ...), custom_call_target="tpu_custom_call" | custom-call | flops 2147483648 | bytes 8388608 | tf_op jit(solution)/shard_map/early/pallas_call | solution.py:135
  122.4 5.6 %decode.1 = bf16[227,1024]{1,0:T(8,128)(2,1)} custom-call(f32[3,1024,16]{2,1,0:T(8,128)S(1)} %get-tuple-element.68.refs_0_, f32[3,1024,512]{2,1,0:T(8,128)S(1)} %early.1.refs_1_, bf16[2,128,512]{2,1,0:T(8,128)(2,1)S(1)} %collective-permute-done.34.refs_2_, bf16[2,128,512]{2,1,0:T(8,128)(2,1)S(1)} %collective-permute-done.35.refs_3_, ...), custom_call_target="tpu_custom_call" | custom-call | flops 2684354560 | bytes 8388608 | tf_op jit(solution)/shard_map/decode/pallas_call | solution.py:135
  (65 shorter events, 19.7 us)
Async XLA Ops:
  1.7 12.9 %collective-permute-start = (bf16[176,512]{1,0:T(8,128)(2,1)S(1)}, bf16[176,512]{1,0:T(8,128)(2,1)S(1)}, u32[]{:S(2)}, u32[]{:S(2)}) collective-permute-start(bf16[176,512]{1,0:T(8,128)(2,1)S(1)} %get-tuple-element.53), channel_id=1, source_target_pairs={{0,1},{1,2},{2,3},{3,4},{4,5},{5,6},{6,7},{7,8},{8,9},{9,10},{10,1... | collective-permute-start | bytes 540680 | tf_op jit(solution)/shard_map/ppermute | solution.py:589
  1.8 12.8 %collective-permute-start.1 = (bf16[176,512]{1,0:T(8,128)(2,1)S(1)}, bf16[176,512]{1,0:T(8,128)(2,1)S(1)}, u32[]{:S(2)}, u32[]{:S(2)}) collective-permute-start(bf16[176,512]{1,0:T(8,128)(2,1)S(1)} %get-tuple-element.53), channel_id=1, source_target_pairs={{0,15},{1,0},{2,1},{3,2},{4,3},{5,4},{6,5},{7,6},{8,7},{9,8},{10,9... | collective-permute-start | bytes 540680 | tf_op jit(solution)/shard_map/ppermute | solution.py:589
  5.6 12.8 %collective-permute-start.2 = (bf16[176,512]{1,0:T(8,128)(2,1)S(1)}, bf16[176,512]{1,0:T(8,128)(2,1)S(1)}, u32[]{:S(2)}, u32[]{:S(2)}) collective-permute-start(bf16[176,512]{1,0:T(8,128)(2,1)S(1)} %get-tuple-element.53), channel_id=1, source_target_pairs={{0,16},{16,0},{32,48},{48,32},{64,80},{80,64},{96,112},{112,96},{1... | collective-permute-start | bytes 540680 | tf_op jit(solution)/shard_map/ppermute | solution.py:596
  6.0 12.4 %collective-permute-start.3 = (bf16[176,512]{1,0:T(8,128)(2,1)S(1)}, bf16[176,512]{1,0:T(8,128)(2,1)S(1)}, u32[]{:S(2)}, u32[]{:S(2)}) collective-permute-start(bf16[176,512]{1,0:T(8,128)(2,1)S(1)} %get-tuple-element.53), channel_id=1, source_target_pairs={{16,32},{48,64},{80,96},{112,0},{32,16},{64,48},{96,80},{0,112},{1... | collective-permute-start | bytes 540680 | tf_op jit(solution)/shard_map/ppermute | solution.py:595
  19.0 12.0 %collective-permute-start.4 = (bf16[2,176,512]{2,1,0:T(8,128)(2,1)S(1)}, bf16[2,176,512]{2,1,0:T(8,128)(2,1)S(1)}, u32[]{:S(2)}, u32[]{:S(2)}) collective-permute-start(bf16[2,176,512]{2,1,0:T(8,128)(2,1)S(1)} %pair.2.refs_3_.refs_4_), channel_id=1, source_target_pairs={{0,1},{1,2},{2,3},{3,4},{4,5},{5,6},{6,7},{7,8},{8,9},{9,10},{10,1... | collective-permute-start | bytes 1081352 | tf_op jit(solution)/shard_map/ppermute | solution.py:589
  19.1 11.9 %collective-permute-start.5 = (bf16[2,176,512]{2,1,0:T(8,128)(2,1)S(1)}, bf16[2,176,512]{2,1,0:T(8,128)(2,1)S(1)}, u32[]{:S(2)}, u32[]{:S(2)}) collective-permute-start(bf16[2,176,512]{2,1,0:T(8,128)(2,1)S(1)} %pair.2.refs_3_.refs_4_), channel_id=1, source_target_pairs={{0,15},{1,0},{2,1},{3,2},{4,3},{5,4},{6,5},{7,6},{8,7},{9,8},{10,9... | collective-permute-start | bytes 1081352 | tf_op jit(solution)/shard_map/ppermute | solution.py:589
  35.3 8.4 %collective-permute-start.10 = (bf16[2,128,512]{2,1,0:T(8,128)(2,1)S(1)}, bf16[2,128,512]{2,1,0:T(8,128)(2,1)S(1)}, u32[]{:S(2)}, u32[]{:S(2)}) collective-permute-start(bf16[2,128,512]{2,1,0:T(8,128)(2,1)S(1)} %get-tuple-element.67.refs_6_), channel_id=1, source_target_pairs={{0,15},{1,0},{2,1},{3,2},{4,3},{5,4},{6,5},{7,6},{8,7},{9,8},{10,9... | collective-permute-start | bytes 786440 | tf_op jit(solution)/shard_map/ppermute | solution.py:589
  37.0 7.9 %collective-permute-start.9 = (bf16[2,128,512]{2,1,0:T(8,128)(2,1)S(1)}, bf16[2,128,512]{2,1,0:T(8,128)(2,1)S(1)}, u32[]{:S(2)}, u32[]{:S(2)}) collective-permute-start(bf16[2,128,512]{2,1,0:T(8,128)(2,1)S(1)} %get-tuple-element.77), channel_id=1, source_target_pairs={{0,1},{1,2},{2,3},{3,4},{4,5},{5,6},{6,7},{7,8},{8,9},{9,10},{10,1... | collective-permute-start | bytes 786440 | tf_op jit(solution)/shard_map/ppermute | solution.py:589
  39.6 18.1 %collective-permute-start.7 = (bf16[128,512]{1,0:T(8,128)(2,1)S(1)}, bf16[128,512]{1,0:T(8,128)(2,1)S(1)}, u32[]{:S(2)}, u32[]{:S(2)}) collective-permute-start(bf16[128,512]{1,0:T(8,128)(2,1)S(1)} %get-tuple-element.73), channel_id=1, source_target_pairs={{0,1},{1,2},{2,3},{3,4},{4,5},{5,6},{6,7},{7,8},{8,9},{9,10},{10,1... | collective-permute-start | bytes 393224 | tf_op jit(solution)/shard_map/ppermute | solution.py:589
  39.7 18.1 %collective-permute-start.8 = (bf16[128,512]{1,0:T(8,128)(2,1)S(1)}, bf16[128,512]{1,0:T(8,128)(2,1)S(1)}, u32[]{:S(2)}, u32[]{:S(2)}) collective-permute-start(bf16[128,512]{1,0:T(8,128)(2,1)S(1)} %get-tuple-element.74), channel_id=1, source_target_pairs={{0,15},{1,0},{2,1},{3,2},{4,3},{5,4},{6,5},{7,6},{8,7},{9,8},{10,9... | collective-permute-start | bytes 393224 | tf_op jit(solution)/shard_map/ppermute | solution.py:589
  45.6 12.1 %collective-permute-start.11 = (bf16[128,512]{1,0:T(8,128)(2,1)S(1)}, bf16[128,512]{1,0:T(8,128)(2,1)S(1)}, u32[]{:S(2)}, u32[]{:S(2)}) collective-permute-start(bf16[128,512]{1,0:T(8,128)(2,1)S(1)} %get-tuple-element.78.refs_6_), channel_id=1, source_target_pairs={{0,16},{16,0},{32,48},{48,32},{64,80},{80,64},{96,112},{112,96},{1... | collective-permute-start | bytes 393224 | tf_op jit(solution)/shard_map/ppermute | solution.py:596
  50.0 9.3 %collective-permute-start.12 = (bf16[128,512]{1,0:T(8,128)(2,1)S(1)}, bf16[128,512]{1,0:T(8,128)(2,1)S(1)}, u32[]{:S(2)}, u32[]{:S(2)}) collective-permute-start(bf16[128,512]{1,0:T(8,128)(2,1)S(1)} %get-tuple-element.79), channel_id=1, source_target_pairs={{16,32},{48,64},{80,96},{32,16},{64,48},{96,80},{17,33},{49,65},{8... | collective-permute-start | bytes 393224 | tf_op jit(solution)/shard_map/ppermute | solution.py:595
  52.5 5.2 %collective-permute-start.6 = (bf16[16,256]{1,0:T(8,128)(2,1)S(1)}, bf16[16,256]{1,0:T(8,128)(2,1)S(1)}, u32[]{:S(2)}, u32[]{:S(2)}) collective-permute-start(bf16[16,256]{1,0:T(8,128)(2,1)S(1)} %get-tuple-element.69.refs_1_), channel_id=1, source_target_pairs={{0,64},{1,65},{2,66},{3,67},{4,68},{5,69},{6,70},{7,71},{8,72},{9,... | collective-permute-start | bytes 24584 | tf_op jit(solution)/shard_map/ppermute | solution.py:793
  60.9 7.2 %collective-permute-start.13 = (bf16[128,512]{1,0:T(8,128)(2,1)S(1)}, bf16[128,512]{1,0:T(8,128)(2,1)S(1)}, u32[]{:S(2)}, u32[]{:S(2)}) collective-permute-start(bf16[128,512]{1,0:T(8,128)(2,1)S(1)} %get-tuple-element.85.refs_3_.refs_1_), channel_id=1, source_target_pairs={{0,16},{16,0},{32,48},{48,32},{64,80},{80,64},{96,112},{112,96},{1... | collective-permute-start | bytes 393224 | tf_op jit(solution)/shard_map/ppermute | solution.py:815
  61.0 7.1 %collective-permute-start.14 = (bf16[16,512]{1,0:T(8,128)(2,1)S(1)}, bf16[16,512]{1,0:T(8,128)(2,1)S(1)}, u32[]{:S(2)}, u32[]{:S(2)}) collective-permute-start(bf16[16,512]{1,0:T(8,128)(2,1)S(1)} %get-tuple-element.86.refs_0_), channel_id=1, source_target_pairs={{0,2},{1,3},{2,0},{3,1},{4,6},{5,7},{6,4},{7,5},{8,10},{9,11},{10,... | collective-permute-start | bytes 49160 | tf_op jit(solution)/shard_map/ppermute | solution.py:816
  62.1 6.0 %collective-permute-start.15 = (bf16[16,512]{1,0:T(8,128)(2,1)S(1)}, bf16[16,512]{1,0:T(8,128)(2,1)S(1)}, u32[]{:S(2)}, u32[]{:S(2)}) collective-permute-start(bf16[16,512]{1,0:T(8,128)(2,1)S(1)} %get-tuple-element.86.refs_0_), channel_id=1, source_target_pairs={{0,18},{1,19},{2,16},{3,17},{4,22},{5,23},{6,20},{7,21},{8,26},{9,... | collective-permute-start | bytes 49160 | tf_op jit(solution)/shard_map/ppermute | solution.py:817
  68.1 11.0 %collective-permute-start.16 = (bf16[128,512]{1,0:T(8,128)(2,1)S(1)}, bf16[128,512]{1,0:T(8,128)(2,1)S(1)}, u32[]{:S(2)}, u32[]{:S(2)}) collective-permute-start(bf16[128,512]{1,0:T(8,128)(2,1)S(1)} %get-tuple-element.88.refs_2_), channel_id=1, source_target_pairs={{0,32},{16,48},{32,64},{48,80},{64,96},{80,112},{96,0},{112,16},{1... | collective-permute-start | bytes 393224 | tf_op jit(solution)/shard_map/ppermute | solution.py:837
  68.3 10.8 %collective-permute-start.17 = (bf16[128,512]{1,0:T(8,128)(2,1)S(1)}, bf16[128,512]{1,0:T(8,128)(2,1)S(1)}, u32[]{:S(2)}, u32[]{:S(2)}) collective-permute-start(bf16[128,512]{1,0:T(8,128)(2,1)S(1)} %get-tuple-element.88.refs_2_), channel_id=1, source_target_pairs={{0,96},{16,112},{32,0},{48,16},{64,32},{80,48},{96,64},{112,80},{1... | collective-permute-start | bytes 393224 | tf_op jit(solution)/shard_map/ppermute | solution.py:838
  71.4 7.0 %collective-permute-start.18 = (bf16[64,512]{1,0:T(8,128)(2,1)S(1)}, bf16[64,512]{1,0:T(8,128)(2,1)S(1)}, u32[]{:S(2)}, u32[]{:S(2)}) collective-permute-start(bf16[64,512]{1,0:T(8,128)(2,1)S(1)} %get-tuple-element.89.refs_5_), channel_id=1, source_target_pairs={{0,4},{1,5},{2,6},{3,7},{4,8},{5,9},{6,10},{7,11},{8,12},{9,13},{1... | collective-permute-start | bytes 196616 | tf_op jit(solution)/shard_map/ppermute | solution.py:836
  72.7 5.8 %collective-permute-start.19 = (bf16[64,512]{1,0:T(8,128)(2,1)S(1)}, bf16[64,512]{1,0:T(8,128)(2,1)S(1)}, u32[]{:S(2)}, u32[]{:S(2)}) collective-permute-start(bf16[64,512]{1,0:T(8,128)(2,1)S(1)} %get-tuple-element.89.refs_5_), channel_id=1, source_target_pairs={{0,8},{1,9},{2,10},{3,11},{4,12},{5,13},{6,14},{7,15},{8,0},{9,1},... | collective-permute-start | bytes 196616 | tf_op jit(solution)/shard_map/ppermute | solution.py:836
  74.8 4.3 %collective-permute-start.20 = (bf16[64,512]{1,0:T(8,128)(2,1)S(1)}, bf16[64,512]{1,0:T(8,128)(2,1)S(1)}, u32[]{:S(2)}, u32[]{:S(2)}) collective-permute-start(bf16[64,512]{1,0:T(8,128)(2,1)S(1)} %get-tuple-element.89.refs_5_), channel_id=1, source_target_pairs={{0,12},{1,13},{2,14},{3,15},{4,0},{5,1},{6,2},{7,3},{8,4},{9,5},{1... | collective-permute-start | bytes 196616 | tf_op jit(solution)/shard_map/ppermute | solution.py:836
  79.7 16.9 %collective-permute-start.21 = (bf16[3,128,512]{2,1,0:T(8,128)(2,1)S(1)}, bf16[3,128,512]{2,1,0:T(8,128)(2,1)S(1)}, u32[]{:S(2)}, u32[]{:S(2)}) collective-permute-start(bf16[3,128,512]{2,1,0:T(8,128)(2,1)S(1)} %get-tuple-element.91.refs_2_), channel_id=1, source_target_pairs={{0,1},{1,2},{2,3},{3,4},{4,5},{5,6},{6,7},{7,8},{8,9},{9,10},{10,1... | collective-permute-start | bytes 1179656 | tf_op jit(solution)/shard_map/ppermute | solution.py:589
  79.8 15.4 %collective-permute-start.23 = (bf16[256,512]{1,0:T(8,128)(2,1)S(1)}, bf16[256,512]{1,0:T(8,128)(2,1)S(1)}, u32[]{:S(2)}, u32[]{:S(2)}) collective-permute-start(bf16[256,512]{1,0:T(8,128)(2,1)S(1)} %get-tuple-element.93.refs_3_), channel_id=1, source_target_pairs={{0,32},{16,48},{32,64},{48,80},{64,96},{80,112},{96,0},{112,16},{1... | collective-permute-start | bytes 786440 | tf_op jit(solution)/shard_map/ppermute | solution.py:847
  79.9 15.8 %collective-permute-start.24 = (bf16[256,512]{1,0:T(8,128)(2,1)S(1)}, bf16[256,512]{1,0:T(8,128)(2,1)S(1)}, u32[]{:S(2)}, u32[]{:S(2)}) collective-permute-start(bf16[256,512]{1,0:T(8,128)(2,1)S(1)} %get-tuple-element.93.refs_3_), channel_id=1, source_target_pairs={{0,64},{16,80},{32,96},{48,112},{64,0},{80,16},{96,32},{112,48},{1... | collective-permute-start | bytes 786440 | tf_op jit(solution)/shard_map/ppermute | solution.py:847
  81.3 15.1 %collective-permute-start.25 = (bf16[256,512]{1,0:T(8,128)(2,1)S(1)}, bf16[256,512]{1,0:T(8,128)(2,1)S(1)}, u32[]{:S(2)}, u32[]{:S(2)}) collective-permute-start(bf16[256,512]{1,0:T(8,128)(2,1)S(1)} %get-tuple-element.93.refs_3_), channel_id=1, source_target_pairs={{0,96},{16,112},{32,0},{48,16},{64,32},{80,48},{96,64},{112,80},{1... | collective-permute-start | bytes 786440 | tf_op jit(solution)/shard_map/ppermute | solution.py:847
  83.1 13.8 %collective-permute-start.22 = (bf16[3,128,512]{2,1,0:T(8,128)(2,1)S(1)}, bf16[3,128,512]{2,1,0:T(8,128)(2,1)S(1)}, u32[]{:S(2)}, u32[]{:S(2)}) collective-permute-start(bf16[3,128,512]{2,1,0:T(8,128)(2,1)S(1)} %get-tuple-element.91.refs_2_), channel_id=1, source_target_pairs={{0,15},{1,0},{2,1},{3,2},{4,3},{5,4},{6,5},{7,6},{8,7},{9,8},{10,9... | collective-permute-start | bytes 1179656 | tf_op jit(solution)/shard_map/ppermute | solution.py:589
  101.3 9.2 %collective-permute-start.32 = (bf16[128,512]{1,0:T(8,128)(2,1)S(1)}, bf16[128,512]{1,0:T(8,128)(2,1)S(1)}, u32[]{:S(2)}, u32[]{:S(2)}) collective-permute-start(bf16[128,512]{1,0:T(8,128)(2,1)S(1)} %mesh.1.refs_3_.refs_2_), channel_id=1, source_target_pairs={{0,16},{16,0},{32,48},{48,32},{64,80},{80,64},{96,112},{112,96},{1... | collective-permute-start | bytes 393224 | tf_op jit(solution)/shard_map/ppermute | solution.py:596
  102.7 10.7 %collective-permute-start.33 = (bf16[128,512]{1,0:T(8,128)(2,1)S(1)}, bf16[128,512]{1,0:T(8,128)(2,1)S(1)}, u32[]{:S(2)}, u32[]{:S(2)}) collective-permute-start(bf16[128,512]{1,0:T(8,128)(2,1)S(1)} %mesh.1.refs_3_.refs_2_), channel_id=1, source_target_pairs={{16,32},{48,64},{80,96},{32,16},{64,48},{96,80},{17,33},{49,65},{8... | collective-permute-start | bytes 393224 | tf_op jit(solution)/shard_map/ppermute | solution.py:595
  106.5 11.3 %collective-permute-start.30 = (bf16[128,512]{1,0:T(8,128)(2,1)S(1)}, bf16[128,512]{1,0:T(8,128)(2,1)S(1)}, u32[]{:S(2)}, u32[]{:S(2)}) collective-permute-start(bf16[128,512]{1,0:T(8,128)(2,1)S(1)} %mesh.1.refs_3_.refs_2_), channel_id=1, source_target_pairs={{0,1},{1,2},{2,3},{3,4},{4,5},{5,6},{6,7},{7,8},{8,9},{9,10},{10,1... | collective-permute-start | bytes 393224 | tf_op jit(solution)/shard_map/ppermute | solution.py:589
  106.6 11.3 %collective-permute-start.31 = (bf16[128,512]{1,0:T(8,128)(2,1)S(1)}, bf16[128,512]{1,0:T(8,128)(2,1)S(1)}, u32[]{:S(2)}, u32[]{:S(2)}) collective-permute-start(bf16[128,512]{1,0:T(8,128)(2,1)S(1)} %mesh.1.refs_3_.refs_2_), channel_id=1, source_target_pairs={{0,15},{1,0},{2,1},{3,2},{4,3},{5,4},{6,5},{7,6},{8,7},{9,8},{10,9... | collective-permute-start | bytes 393224 | tf_op jit(solution)/shard_map/ppermute | solution.py:589
  113.9 8.5 %collective-permute-start.34 = (bf16[2,128,512]{2,1,0:T(8,128)(2,1)S(1)}, bf16[2,128,512]{2,1,0:T(8,128)(2,1)S(1)}, u32[]{:S(2)}, u32[]{:S(2)}) collective-permute-start(bf16[2,128,512]{2,1,0:T(8,128)(2,1)S(1)} %pair.3.refs_4_), channel_id=1, source_target_pairs={{0,1},{1,2},{2,3},{3,4},{4,5},{5,6},{6,7},{7,8},{8,9},{9,10},{10,1... | collective-permute-start | bytes 786440 | tf_op jit(solution)/shard_map/ppermute | solution.py:589
  114.0 8.4 %collective-permute-start.35 = (bf16[2,128,512]{2,1,0:T(8,128)(2,1)S(1)}, bf16[2,128,512]{2,1,0:T(8,128)(2,1)S(1)}, u32[]{:S(2)}, u32[]{:S(2)}) collective-permute-start(bf16[2,128,512]{2,1,0:T(8,128)(2,1)S(1)} %pair.3.refs_4_), channel_id=1, source_target_pairs={{0,15},{1,0},{2,1},{3,2},{4,3},{5,4},{6,5},{7,6},{8,7},{9,8},{10,9... | collective-permute-start | bytes 786440 | tf_op jit(solution)/shard_map/ppermute | solution.py:589
  (5 other events, 15.5 us)
where the time goes:
time: 130 us; the launch traced here: 128 us
  starting transfers between devices  59.7 us (46%)
  Pallas kernels  48.6 us (37%)
  waiting for transfers between devices  18.5 us (14%)
    pallas_call x22, Pallas kernels, kernel_call(): pl.pallas_call(run, out_shape=outs, in_specs=[HBM if isinstance(q, Load)...  48.6 us
    ppermute x14, starting transfers between devices, shift(): return lax.ppermute(value, axis, pairs)  24.7 us
    ppermute x3, starting transfers between devices, swap_bands(): second = lax.ppermute(second, 'lat', later)  10.8 us
    ppermute x3, waiting for transfers between devices, per_device(): lax.ppermute(rows, 'lat', along_z(s))  9.59 us
    ppermute x3, starting transfers between devices, swap_bands(): return (lax.ppermute(first, 'lat', [(i, i ^ 1) for i in range(8)]), second)  6.16 us
    ppermute x3, starting transfers between devices, per_device(): lax.ppermute(beside, 'lon', along_y(s))  5.3 us
    ppermute x3, waiting for transfers between devices, swap_bands(): second = lax.ppermute(second, 'lat', later)  4.38 us
    ppermute x3, starting transfers between devices, per_device(): lax.ppermute(rows, 'lat', along_z(s))  3.3 us
  transfers between devices with their start and end apart: 36, of which 10 were waited for; matrix products, arithmetic and copies ran while one was open for 0% of the time, Pallas kernels for 25%

commit v1 on v0

--- a/solution.py
+++ b/solution.py
@@ -567,18 +567,16 @@
 def decode_body(edges, early, left_pair, right_pair, base, folded, head, out, rows, totals):
     for k, part in enumerate((left_pair.at[0], left_pair.at[1], right_pair.at[0], right_pair.at[1])):
         rows[MESH_NODES * k : MESH_NODES * (k + 1), :] = part[...]
-    @pl.loop(0, 4)
-    def _(b):
-        span = pl.ds(pl.multiple_of(256 * b, 256), 256)
+    for b in range(4):
+        span = slice(256 * b, 256 * (b + 1))
         total = jnp.zeros((256, WIDTH), F32)
         for t in range(GRID_DEGREE):
             spot = edges[t, span, :][:, 0:1].astype(I32) - 5 * MESH_NODES
             total += silu(early[t, span, :] + mm(one_hot(spot, 4 * MESH_NODES), rows[...]))
         totals[span, :] = total.astype(BF)
 
-    @pl.loop(0, 2)
-    def _(b):
-        span = pl.ds(pl.multiple_of(512 * b, 512), 512)
+    for b in range(2):
+        span = slice(512 * b, 512 * (b + 1))
         hidden = silu(base[span, :] + mm(totals[span, :], folded[...])).astype(BF)
         out[:, span] = mm_nt(head[...], hidden).astype(BF)
 

time: 130 us -> 129 us (level)
  no operation moved by 1% of the time
where the time goes in v1:
time: 129 us; the launch traced here: 127 us
  starting transfers between devices  59.7 us (46%)
  Pallas kernels  47.6 us (37%)
  waiting for transfers between devices  18.5 us (14%)
    pallas_call x22, Pallas kernels, kernel_call(): pl.pallas_call(run, out_shape=outs, in_specs=[HBM if isinstance(q, Load)...  47.6 us
    ppermute x14, starting transfers between devices, shift(): return lax.ppermute(value, axis, pairs)  24.7 us
    ppermute x3, starting transfers between devices, swap_bands(): second = lax.ppermute(second, 'lat', later)  10.8 us
    ppermute x3, waiting for transfers between devices, per_device(): lax.ppermute(rows, 'lat', along_z(s))  9.59 us
    ppermute x3, starting transfers between devices, swap_bands(): return (lax.ppermute(first, 'lat', [(i, i ^ 1) for i in range(8)]), second)  6.16 us
    ppermute x3, starting transfers between devices, per_device(): lax.ppermute(beside, 'lon', along_y(s))  5.3 us
    ppermute x3, waiting for transfers between devices, swap_bands(): second = lax.ppermute(second, 'lat', later)  4.38 us
    ppermute x3, starting transfers between devices, per_device(): lax.ppermute(rows, 'lat', along_z(s))  3.3 us
  transfers between devices with their start and end apart: 36, of which 10 were waited for; matrix products, arithmetic and copies ran while one was open for 0% of the time, Pallas kernels for 25%

profile of v1, /device:TPU:4, one launch (start us, length us, event | category | flops | bytes accessed | tf_op | source)
XLA Modules:
  0.0 127.0 jit_solution(6376893084210920916)
XLA Ops:
  1.8 3.8 %collective-permute-start.1 = (bf16[176,512]{1,0:T(8,128)(2,1)S(1)}, bf16[176,512]{1,0:T(8,128)(2,1)S(1)}, u32[]{:S(2)}, u32[]{:S(2)}) collective-permute-start(bf16[176,512]{1,0:T(8,128)(2,1)S(1)} %get-tuple-element.53), channel_id=1, source_target_pairs={{0,15},{1,0},{2,1},{3,2},{4,3},{5,4},{6,5},{7,6},{8,7},{9,8},{10,9... | collective-permute-start | bytes 540680 | tf_op jit(solution)/shard_map/ppermute | solution.py:587
  6.0 4.5 %collective-permute-start.3 = (bf16[176,512]{1,0:T(8,128)(2,1)S(1)}, bf16[176,512]{1,0:T(8,128)(2,1)S(1)}, u32[]{:S(2)}, u32[]{:S(2)}) collective-permute-start(bf16[176,512]{1,0:T(8,128)(2,1)S(1)} %get-tuple-element.53), channel_id=1, source_target_pairs={{16,32},{48,64},{80,96},{112,0},{32,16},{64,48},{96,80},{0,112},{1... | collective-permute-start | bytes 540680 | tf_op jit(solution)/shard_map/ppermute | solution.py:593
  10.5 3.9 %embed.1 = (bf16[1024,512]{1,0:T(8,128)(2,1)S(1)}, bf16[512,512]{1,0:T(8,128)(2,1)S(1)}) custom-call(bf16[1,1,474,1024]{3,2,1,0:T(8,128)(2,1)} %bitcast.19, bf16[474,512]{1,0:T(8,128)(2,1)} %refs_1_.6, bf16[512,512]{1,0:T(8,128)(2,1)} %refs_2_.6, bf16[3,3,512,512]{3,2,1,0:T(8,128)(2,1)} %refs_1_.9), custom_call_target="tpu_custom_call" | custom-call | flops 1073741824 | bytes 4194304 | tf_op jit(solution)/shard_map/embed/pallas_call | solution.py:135
  15.5 2.9 %own_first.1 = (f32[128,512]{1,0:T(8,128)S(1)}, bf16[32,512]{1,0:T(8,128)(2,1)S(1)}) custom-call(bf16[1,1,128,512]{3,2,1,0:T(8,128)(2,1)} %refs_5_.5, bf16[64,512]{1,0:T(8,128)(2,1)S(1)} %get-tuple-element.54.refs_1_, bf16[1024,512]{1,0:T(8,128)(2,1)S(1)} %send.1.refs_2_.refs_5_.refs_8_, bf16[3,3,512,512]{3,2,1,0:T(8,128)(2,1)} %refs_1_.9, ...), custom_call_target="tpu_custom_call" | custom-call | flops 1073741824 | bytes 3145728 | tf_op jit(solution)/shard_map/own_first/pallas_call | solution.py:135
  19.1 3.8 %collective-permute-start.5 = (bf16[2,176,512]{2,1,0:T(8,128)(2,1)S(1)}, bf16[2,176,512]{2,1,0:T(8,128)(2,1)S(1)}, u32[]{:S(2)}, u32[]{:S(2)}) collective-permute-start(bf16[2,176,512]{2,1,0:T(8,128)(2,1)S(1)} %pair.2.refs_3_.refs_4_), channel_id=1, source_target_pairs={{0,15},{1,0},{2,1},{3,2},{4,3},{5,4},{6,5},{7,6},{8,7},{9,8},{10,9... | collective-permute-start | bytes 1081352 | tf_op jit(solution)/shard_map/ppermute | solution.py:587
  22.9 3.0 %own_last.1.refs_6_.refs_0_ = f32[128,512]{1,0:T(8,128)S(1)} custom-call(bf16[1,1,128,512]{3,2,1,0:T(8,128)(2,1)} %refs_5_.5, bf16[32,512]{1,0:T(8,128)(2,1)S(1)} %get-tuple-element.62.refs_1_, bf16[1024,512]{1,0:T(8,128)(2,1)S(1)} %send.1.refs_2_.refs_5_.refs_8_, bf16[3,3,512,512]{3,2,1,0:T(8,128)(2,1)} %refs_1_.9, ...), custom_call_target="tpu_custom_call" | custom-call | flops 1073741824 | bytes 3145728 | tf_op jit(solution)/shard_map/own_last/pallas_call | solution.py:135
  25.9 4.4 %beside.1 = (bf16[128,512]{1,0:T(8,128)(2,1)S(1)}, bf16[128,512]{1,0:T(8,128)(2,1)S(1)}, bf16[128,512]{1,0:T(8,128)(2,1)S(1)}, bf16[128,512]{1,0:T(8,128)(2,1)S(1)}, bf16[16,256]{1,0:T(8,128)(2,1)S(1)}) custom-call(s32[1,5]{1,0:T(1,128)S(1)} %bitcast.13, bf16[176,512]{1,0:T(8,128)(2,1)S(1)} %collective-permute-done.refs_2_.refs_1_, ...), custom_call_target="tpu_custom_call" | custom-call | flops 1073741824 | bytes 5242880 | tf_op jit(solution)/shard_map/beside/pallas_call | solution.py:135
  31.0 4.2 %corners.1 = (bf16[128,512]{1,0:T(8,128)(2,1)S(1)}, bf16[128,512]{1,0:T(8,128)(2,1)S(1)}, bf16[128,512]{1,0:T(8,128)(2,1)S(1)}, bf16[128,512]{1,0:T(8,128)(2,1)S(1)}, bf16[16,256]{1,0:T(8,128)(2,1)S(1)}) custom-call(s32[1,5]{1,0:T(1,128)S(1)} %bitcast.14, bf16[2,176,512]{2,1,0:T(8,128)(2,1)S(1)} %collective-permute-done.4.refs_1_.refs_2_, ...), custom_call_target="tpu_custom_call" | custom-call | flops 1073741824 | bytes 5242880 | tf_op jit(solution)/shard_map/corners/pallas_call | solution.py:135
  35.3 1.8 %collective-permute-start.10 = (bf16[2,128,512]{2,1,0:T(8,128)(2,1)S(1)}, bf16[2,128,512]{2,1,0:T(8,128)(2,1)S(1)}, u32[]{:S(2)}, u32[]{:S(2)}) collective-permute-start(bf16[2,128,512]{2,1,0:T(8,128)(2,1)S(1)} %get-tuple-element.67.refs_6_), channel_id=1, source_target_pairs={{0,15},{1,0},{2,1},{3,2},{4,3},{5,4},{6,5},{7,6},{8,7},{9,8},{10,9... | collective-permute-start | bytes 786440 | tf_op jit(solution)/shard_map/ppermute | solution.py:587
  37.0 2.5 %prep.1 = (f32[6,128,16]{2,1,0:T(8,128)S(1)}, f32[3,1024,16]{2,1,0:T(8,128)S(1)}, bf16[128,512]{1,0:T(8,128)(2,1)S(1)}, bf16[128,512]{1,0:T(8,128)(2,1)S(1)}, bf...) custom-call(s32[1,1,768]{2,1,0:T(1,128)} %refs_0_.7, ...), custom_call_target="tpu_custom_call" | custom-call | flops 536870912 | tf_op jit(solution)/shard_map/prep/pallas_call | solution.py:135
  39.7 3.9 %collective-permute-start.8 = (bf16[128,512]{1,0:T(8,128)(2,1)S(1)}, bf16[128,512]{1,0:T(8,128)(2,1)S(1)}, u32[]{:S(2)}, u32[]{:S(2)}) collective-permute-start(bf16[128,512]{1,0:T(8,128)(2,1)S(1)} %get-tuple-element.74), channel_id=1, source_target_pairs={{0,15},{1,0},{2,1},{3,2},{4,3},{5,4},{6,5},{7,6},{8,7},{9,8},{10,9... | collective-permute-start | bytes 393224 | tf_op jit(solution)/shard_map/ppermute | solution.py:587
  45.6 4.3 %collective-permute-start.11 = (bf16[128,512]{1,0:T(8,128)(2,1)S(1)}, bf16[128,512]{1,0:T(8,128)(2,1)S(1)}, u32[]{:S(2)}, u32[]{:S(2)}) collective-permute-start(bf16[128,512]{1,0:T(8,128)(2,1)S(1)} %get-tuple-element.78.refs_6_), channel_id=1, source_target_pairs={{0,16},{16,0},{32,48},{48,32},{64,80},{80,64},{96,112},{112,96},{1... | collective-permute-start | bytes 393224 | tf_op jit(solution)/shard_map/ppermute | solution.py:594
  50.0 2.5 %collective-permute-start.12 = (bf16[128,512]{1,0:T(8,128)(2,1)S(1)}, bf16[128,512]{1,0:T(8,128)(2,1)S(1)}, u32[]{:S(2)}, u32[]{:S(2)}) collective-permute-start(bf16[128,512]{1,0:T(8,128)(2,1)S(1)} %get-tuple-element.79), channel_id=1, source_target_pairs={{16,32},{48,64},{80,96},{32,16},{64,48},{96,80},{17,33},{49,65},{8... | collective-permute-start | bytes 393224 | tf_op jit(solution)/shard_map/ppermute | solution.py:593
  53.4 2.6 %fold.1 = (bf16[512,512]{1,0:T(8,128)(2,1)S(1)}, bf16[512,512]{1,0:T(8,128)(2,1)S(1)}, bf16[512,512]{1,0:T(8,128)(2,1)S(1)}) custom-call(bf16[3,3,512,512]{3,2,1,0:T(8,128)(2,1)} %refs_1_.9, bf16[3,1024,512]{2,1,0:T(8,128)(2,1)} %refs_2_.9, bf16[3,3,512,512]{3,2,1,0:T(8,128)(2,1)} %refs_1_.9, bf16[3,1024,512]{2,1,0:T(8,128)(2,1)} %refs_2_.9, ...), custom_call_target="tpu_custom_call" | custom-call | flops 805306368 | bytes 4194304 | tf_op jit(solution)/shard_map/fold/pallas_call | solution.py:135
  59.2 1.7 %node.1 = (bf16[128,512]{1,0:T(8,128)(2,1)S(1)}, bf16[128,512]{1,0:T(8,128)(2,1)S(1)}, bf16[128,512]{1,0:T(8,128)(2,1)S(1)}, bf16[16,512]{1,0:T(8,128)(2,1)S(1)}) custom-call(f32[128,512]{1,0:T(8,128)S(1)} %own_last.1.refs_6_.refs_0_, bf16[128,512]{1,0:T(8,128)(2,1)S(1)} %collective-permute-done.7.refs_1_, ...), custom_call_target="tpu_custom_call" | custom-call | flops 469762048 | bytes 4194304 | tf_op jit(solution)/shard_map/node/pallas_call | solution.py:135
  62.1 3.0 %collective-permute-start.15 = (bf16[16,512]{1,0:T(8,128)(2,1)S(1)}, bf16[16,512]{1,0:T(8,128)(2,1)S(1)}, u32[]{:S(2)}, u32[]{:S(2)}) collective-permute-start(bf16[16,512]{1,0:T(8,128)(2,1)S(1)} %get-tuple-element.86.refs_0_), channel_id=1, source_target_pairs={{0,18},{1,19},{2,16},{3,17},{4,22},{5,23},{6,20},{7,21},{8,26},{9,... | collective-permute-start | bytes 49160 | tf_op jit(solution)/shard_map/ppermute | solution.py:815
  65.1 3.0 %grid.1 = (bf16[1024,512]{1,0:T(8,128)(2,1)S(1)}, f32[1024,512]{1,0:T(8,128)S(1)}) custom-call(bf16[1024,512]{1,0:T(8,128)(2,1)S(1)} %get-tuple-element.55.refs_0_, bf16[3,3,512,512]{3,2,1,0:T(8,128)(2,1)} %refs_1_.9, bf16[3,1024,512]{2,1,0:T(8,128)(2,1)} %refs_2_.9, bf16[128,512]{1,0:T(8,128)(2,1)S(1)} %get-tuple-element.85.refs_3_.refs_1_), custom_call_target="tpu_custom_call" | custom-call | flops 1073741824 | bytes 5242880 | tf_op jit(solution)/shard_map/grid/pallas_call | solution.py:135
  68.3 3.1 %collective-permute-start.17 = (bf16[128,512]{1,0:T(8,128)(2,1)S(1)}, bf16[128,512]{1,0:T(8,128)(2,1)S(1)}, u32[]{:S(2)}, u32[]{:S(2)}) collective-permute-start(bf16[128,512]{1,0:T(8,128)(2,1)S(1)} %get-tuple-element.88.refs_2_), channel_id=1, source_target_pairs={{0,96},{16,112},{32,0},{48,16},{64,32},{80,48},{96,64},{112,80},{1... | collective-permute-start | bytes 393224 | tf_op jit(solution)/shard_map/ppermute | solution.py:836
  72.7 2.1 %collective-permute-start.19 = (bf16[64,512]{1,0:T(8,128)(2,1)S(1)}, bf16[64,512]{1,0:T(8,128)(2,1)S(1)}, u32[]{:S(2)}, u32[]{:S(2)}) collective-permute-start(bf16[64,512]{1,0:T(8,128)(2,1)S(1)} %get-tuple-element.89.refs_5_), channel_id=1, source_target_pairs={{0,8},{1,9},{2,10},{3,11},{4,12},{5,13},{6,14},{7,15},{8,0},{9,1},... | collective-permute-start | bytes 196616 | tf_op jit(solution)/shard_map/ppermute | solution.py:834
  74.8 1.9 %collective-permute-start.20 = (bf16[64,512]{1,0:T(8,128)(2,1)S(1)}, bf16[64,512]{1,0:T(8,128)(2,1)S(1)}, u32[]{:S(2)}, u32[]{:S(2)}) collective-permute-start(bf16[64,512]{1,0:T(8,128)(2,1)S(1)} %get-tuple-element.89.refs_5_), channel_id=1, source_target_pairs={{0,12},{1,13},{2,14},{3,15},{4,0},{5,1},{6,2},{7,3},{8,4},{9,5},{1... | collective-permute-start | bytes 196616 | tf_op jit(solution)/shard_map/ppermute | solution.py:834
  76.7 1.7 %coarse_edges.1 = (f32[768,16]{1,0:T(8,128)S(1)}, s32[1,1]{1,0:T(1,128)}) custom-call(s32[1,5]{1,0:T(1,128)S(1)} %bitcast.16, bf16[16,256]{1,0:T(8,128)(2,1)S(1)} %get-tuple-element.69.refs_1_, bf16[16,256]{1,0:T(8,128)(2,1)S(1)} %get-tuple-element.70.refs_2_, bf16[16,256]{1,0:T(8,128)(2,1)S(1)} %collective-permute-done.6.refs_3_.refs_11_), custom_call_target="tpu_custom_call" | custom-call | flops 67108864 | tf_op jit(solution)/shard_map/coarse_edges/pallas_call | solution.py:135
  81.3 1.8 %collective-permute-start.25 = (bf16[256,512]{1,0:T(8,128)(2,1)S(1)}, bf16[256,512]{1,0:T(8,128)(2,1)S(1)}, u32[]{:S(2)}, u32[]{:S(2)}) collective-permute-start(bf16[256,512]{1,0:T(8,128)(2,1)S(1)} %get-tuple-element.93.refs_3_), channel_id=1, source_target_pairs={{0,96},{16,112},{32,0},{48,16},{64,32},{80,48},{96,64},{112,80},{1... | collective-permute-start | bytes 786440 | tf_op jit(solution)/shard_map/ppermute | solution.py:845
  83.1 3.2 %collective-permute-start.22 = (bf16[3,128,512]{2,1,0:T(8,128)(2,1)S(1)}, bf16[3,128,512]{2,1,0:T(8,128)(2,1)S(1)}, u32[]{:S(2)}, u32[]{:S(2)}) collective-permute-start(bf16[3,128,512]{2,1,0:T(8,128)(2,1)S(1)} %get-tuple-element.91.refs_2_), channel_id=1, source_target_pairs={{0,15},{1,0},{2,1},{3,2},{4,3},{5,4},{6,5},{7,6},{8,7},{9,8},{10,9... | collective-permute-start | bytes 1179656 | tf_op jit(solution)/shard_map/ppermute | solution.py:587
  86.3 8.9 %collective-permute-done.23.refs_6_.refs_4_ = bf16[256,512]{1,0:T(8,128)(2,1)S(1)} collective-permute-done((bf16[256,512]{1,0:T(8,128)(2,1)S(1)}, bf16[256,512]{1,0:T(8,128)(2,1)S(1)}, u32[]{:S(2)}, u32[]{:S(2)}) %collective-permute-start.23) | collective-permute-done | bytes 262176 | tf_op jit(solution)/shard_map/ppermute | solution.py:845
  96.9 1.7 %fine.1.refs_1_ = f32[128,512]{1,0:T(8,128)S(1)} custom-call(f32[6,128,16]{2,1,0:T(8,128)S(1)} %get-tuple-element.72.refs_5_.refs_0_, bf16[3,128,512]{2,1,0:T(8,128)(2,1)S(1)} %collective-permute-done.21.refs_1_, bf16[3,128,512]{2,1,0:T(8,128)(2,1)S(1)} %get-tuple-element.91.refs_2_, bf16[3,128,512]{2,1,0:T(8,128)(2,1)S(1)} %collective-permute-done.22.refs_3_, ...), custom_call_target="tpu_custom_call" | custom-call | flops 1073741824 | bytes 3145728 | tf_op jit(solution)/shard_map/fine/pallas_call | solution.py:135
  98.7 2.5 %mesh.1.refs_3_.refs_2_ = bf16[128,512]{1,0:T(8,128)(2,1)S(1)} custom-call(s32[1,1]{1,0:T(1,128)} %get-tuple-element.71.refs_0_, f32[128,512]{1,0:T(8,128)S(1)} %fine.1.refs_1_, f32[768,16]{1,0:T(8,128)S(1)} %get-tuple-element.90.refs_9_.refs_7_.refs_2_, bf16[256,512]{1,0:T(8,128)(2,1)S(1)} %get-tuple-element.93.refs_3_, ...), custom_call_target="tpu_custom_call" | custom-call | flops 2147483648 | bytes 6291456 | tf_op jit(solution)/shard_map/mesh/pallas_call | solution.py:135
  102.7 3.8 %collective-permute-start.33 = (bf16[128,512]{1,0:T(8,128)(2,1)S(1)}, bf16[128,512]{1,0:T(8,128)(2,1)S(1)}, u32[]{:S(2)}, u32[]{:S(2)}) collective-permute-start(bf16[128,512]{1,0:T(8,128)(2,1)S(1)} %mesh.1.refs_3_.refs_2_), channel_id=1, source_target_pairs={{16,32},{48,64},{80,96},{32,16},{64,48},{96,80},{17,33},{49,65},{8... | collective-permute-start | bytes 393224 | tf_op jit(solution)/shard_map/ppermute | solution.py:593
  106.6 3.8 %collective-permute-start.31 = (bf16[128,512]{1,0:T(8,128)(2,1)S(1)}, bf16[128,512]{1,0:T(8,128)(2,1)S(1)}, u32[]{:S(2)}, u32[]{:S(2)}) collective-permute-start(bf16[128,512]{1,0:T(8,128)(2,1)S(1)} %mesh.1.refs_3_.refs_2_), channel_id=1, source_target_pairs={{0,15},{1,0},{2,1},{3,2},{4,3},{5,4},{6,5},{7,6},{8,7},{9,8},{10,9... | collective-permute-start | bytes 393224 | tf_op jit(solution)/shard_map/ppermute | solution.py:587
  110.4 2.9 %collective-permute-done.33.refs_2_ = bf16[128,512]{1,0:T(8,128)(2,1)S(1)} collective-permute-done((bf16[128,512]{1,0:T(8,128)(2,1)S(1)}, bf16[128,512]{1,0:T(8,128)(2,1)S(1)}, u32[]{:S(2)}, u32[]{:S(2)}) %collective-permute-start.33) | collective-permute-done | bytes 131104 | tf_op jit(solution)/shard_map/ppermute | solution.py:593
  114.0 3.8 %collective-permute-start.35 = (bf16[2,128,512]{2,1,0:T(8,128)(2,1)S(1)}, bf16[2,128,512]{2,1,0:T(8,128)(2,1)S(1)}, u32[]{:S(2)}, u32[]{:S(2)}) collective-permute-start(bf16[2,128,512]{2,1,0:T(8,128)(2,1)S(1)} %pair.3.refs_4_), channel_id=1, source_target_pairs={{0,15},{1,0},{2,1},{3,2},{4,3},{5,4},{6,5},{7,6},{8,7},{9,8},{10,9... | collective-permute-start | bytes 786440 | tf_op jit(solution)/shard_map/ppermute | solution.py:587
  117.9 4.5 %early.1.refs_1_ = f32[3,1024,512]{2,1,0:T(8,128)S(1)} custom-call(f32[3,1024,16]{2,1,0:T(8,128)S(1)} %get-tuple-element.68.refs_0_, bf16[128,512]{1,0:T(8,128)(2,1)S(1)} %collective-permute-done.30.refs_1_, bf16[128,512]{1,0:T(8,128)(2,1)S(1)} %mesh.1.refs_3_.refs_2_, bf16[128,512]{1,0:T(8,128)(2,1)S(1)} %collective-permute-done.31.refs_3_, ...), custom_call_target="tpu_custom_call" | custom-call | flops 2147483648 | bytes 8388608 | tf_op jit(solution)/shard_map/early/pallas_call | solution.py:135
  122.4 4.6 %decode.1 = bf16[227,1024]{1,0:T(8,128)(2,1)} custom-call(f32[3,1024,16]{2,1,0:T(8,128)S(1)} %get-tuple-element.68.refs_0_, f32[3,1024,512]{2,1,0:T(8,128)S(1)} %early.1.refs_1_, bf16[2,128,512]{2,1,0:T(8,128)(2,1)S(1)} %collective-permute-done.34.refs_2_, bf16[2,128,512]{2,1,0:T(8,128)(2,1)S(1)} %collective-permute-done.35.refs_3_, ...), custom_call_target="tpu_custom_call" | custom-call | flops 2684354560 | bytes 8388608 | tf_op jit(solution)/shard_map/decode/pallas_call | solution.py:135
  (65 shorter events, 19.7 us)
Async XLA Ops:
  1.7 12.9 %collective-permute-start = (bf16[176,512]{1,0:T(8,128)(2,1)S(1)}, bf16[176,512]{1,0:T(8,128)(2,1)S(1)}, u32[]{:S(2)}, u32[]{:S(2)}) collective-permute-start(bf16[176,512]{1,0:T(8,128)(2,1)S(1)} %get-tuple-element.53), channel_id=1, source_target_pairs={{0,1},{1,2},{2,3},{3,4},{4,5},{5,6},{6,7},{7,8},{8,9},{9,10},{10,1... | collective-permute-start | bytes 540680 | tf_op jit(solution)/shard_map/ppermute | solution.py:587
  1.8 12.8 %collective-permute-start.1 = (bf16[176,512]{1,0:T(8,128)(2,1)S(1)}, bf16[176,512]{1,0:T(8,128)(2,1)S(1)}, u32[]{:S(2)}, u32[]{:S(2)}) collective-permute-start(bf16[176,512]{1,0:T(8,128)(2,1)S(1)} %get-tuple-element.53), channel_id=1, source_target_pairs={{0,15},{1,0},{2,1},{3,2},{4,3},{5,4},{6,5},{7,6},{8,7},{9,8},{10,9... | collective-permute-start | bytes 540680 | tf_op jit(solution)/shard_map/ppermute | solution.py:587
  5.6 12.8 %collective-permute-start.2 = (bf16[176,512]{1,0:T(8,128)(2,1)S(1)}, bf16[176,512]{1,0:T(8,128)(2,1)S(1)}, u32[]{:S(2)}, u32[]{:S(2)}) collective-permute-start(bf16[176,512]{1,0:T(8,128)(2,1)S(1)} %get-tuple-element.53), channel_id=1, source_target_pairs={{0,16},{16,0},{32,48},{48,32},{64,80},{80,64},{96,112},{112,96},{1... | collective-permute-start | bytes 540680 | tf_op jit(solution)/shard_map/ppermute | solution.py:594
  6.0 12.4 %collective-permute-start.3 = (bf16[176,512]{1,0:T(8,128)(2,1)S(1)}, bf16[176,512]{1,0:T(8,128)(2,1)S(1)}, u32[]{:S(2)}, u32[]{:S(2)}) collective-permute-start(bf16[176,512]{1,0:T(8,128)(2,1)S(1)} %get-tuple-element.53), channel_id=1, source_target_pairs={{16,32},{48,64},{80,96},{112,0},{32,16},{64,48},{96,80},{0,112},{1... | collective-permute-start | bytes 540680 | tf_op jit(solution)/shard_map/ppermute | solution.py:593
  19.0 12.0 %collective-permute-start.4 = (bf16[2,176,512]{2,1,0:T(8,128)(2,1)S(1)}, bf16[2,176,512]{2,1,0:T(8,128)(2,1)S(1)}, u32[]{:S(2)}, u32[]{:S(2)}) collective-permute-start(bf16[2,176,512]{2,1,0:T(8,128)(2,1)S(1)} %pair.2.refs_3_.refs_4_), channel_id=1, source_target_pairs={{0,1},{1,2},{2,3},{3,4},{4,5},{5,6},{6,7},{7,8},{8,9},{9,10},{10,1... | collective-permute-start | bytes 1081352 | tf_op jit(solution)/shard_map/ppermute | solution.py:587
  19.1 11.9 %collective-permute-start.5 = (bf16[2,176,512]{2,1,0:T(8,128)(2,1)S(1)}, bf16[2,176,512]{2,1,0:T(8,128)(2,1)S(1)}, u32[]{:S(2)}, u32[]{:S(2)}) collective-permute-start(bf16[2,176,512]{2,1,0:T(8,128)(2,1)S(1)} %pair.2.refs_3_.refs_4_), channel_id=1, source_target_pairs={{0,15},{1,0},{2,1},{3,2},{4,3},{5,4},{6,5},{7,6},{8,7},{9,8},{10,9... | collective-permute-start | bytes 1081352 | tf_op jit(solution)/shard_map/ppermute | solution.py:587
  35.3 8.4 %collective-permute-start.10 = (bf16[2,128,512]{2,1,0:T(8,128)(2,1)S(1)}, bf16[2,128,512]{2,1,0:T(8,128)(2,1)S(1)}, u32[]{:S(2)}, u32[]{:S(2)}) collective-permute-start(bf16[2,128,512]{2,1,0:T(8,128)(2,1)S(1)} %get-tuple-element.67.refs_6_), channel_id=1, source_target_pairs={{0,15},{1,0},{2,1},{3,2},{4,3},{5,4},{6,5},{7,6},{8,7},{9,8},{10,9... | collective-permute-start | bytes 786440 | tf_op jit(solution)/shard_map/ppermute | solution.py:587
  37.0 7.9 %collective-permute-start.9 = (bf16[2,128,512]{2,1,0:T(8,128)(2,1)S(1)}, bf16[2,128,512]{2,1,0:T(8,128)(2,1)S(1)}, u32[]{:S(2)}, u32[]{:S(2)}) collective-permute-start(bf16[2,128,512]{2,1,0:T(8,128)(2,1)S(1)} %get-tuple-element.77), channel_id=1, source_target_pairs={{0,1},{1,2},{2,3},{3,4},{4,5},{5,6},{6,7},{7,8},{8,9},{9,10},{10,1... | collective-permute-start | bytes 786440 | tf_op jit(solution)/shard_map/ppermute | solution.py:587
  39.6 18.1 %collective-permute-start.7 = (bf16[128,512]{1,0:T(8,128)(2,1)S(1)}, bf16[128,512]{1,0:T(8,128)(2,1)S(1)}, u32[]{:S(2)}, u32[]{:S(2)}) collective-permute-start(bf16[128,512]{1,0:T(8,128)(2,1)S(1)} %get-tuple-element.73), channel_id=1, source_target_pairs={{0,1},{1,2},{2,3},{3,4},{4,5},{5,6},{6,7},{7,8},{8,9},{9,10},{10,1... | collective-permute-start | bytes 393224 | tf_op jit(solution)/shard_map/ppermute | solution.py:587
  39.7 18.1 %collective-permute-start.8 = (bf16[128,512]{1,0:T(8,128)(2,1)S(1)}, bf16[128,512]{1,0:T(8,128)(2,1)S(1)}, u32[]{:S(2)}, u32[]{:S(2)}) collective-permute-start(bf16[128,512]{1,0:T(8,128)(2,1)S(1)} %get-tuple-element.74), channel_id=1, source_target_pairs={{0,15},{1,0},{2,1},{3,2},{4,3},{5,4},{6,5},{7,6},{8,7},{9,8},{10,9... | collective-permute-start | bytes 393224 | tf_op jit(solution)/shard_map/ppermute | solution.py:587
  45.6 12.1 %collective-permute-start.11 = (bf16[128,512]{1,0:T(8,128)(2,1)S(1)}, bf16[128,512]{1,0:T(8,128)(2,1)S(1)}, u32[]{:S(2)}, u32[]{:S(2)}) collective-permute-start(bf16[128,512]{1,0:T(8,128)(2,1)S(1)} %get-tuple-element.78.refs_6_), channel_id=1, source_target_pairs={{0,16},{16,0},{32,48},{48,32},{64,80},{80,64},{96,112},{112,96},{1... | collective-permute-start | bytes 393224 | tf_op jit(solution)/shard_map/ppermute | solution.py:594
  50.0 9.3 %collective-permute-start.12 = (bf16[128,512]{1,0:T(8,128)(2,1)S(1)}, bf16[128,512]{1,0:T(8,128)(2,1)S(1)}, u32[]{:S(2)}, u32[]{:S(2)}) collective-permute-start(bf16[128,512]{1,0:T(8,128)(2,1)S(1)} %get-tuple-element.79), channel_id=1, source_target_pairs={{16,32},{48,64},{80,96},{32,16},{64,48},{96,80},{17,33},{49,65},{8... | collective-permute-start | bytes 393224 | tf_op jit(solution)/shard_map/ppermute | solution.py:593
  52.5 5.2 %collective-permute-start.6 = (bf16[16,256]{1,0:T(8,128)(2,1)S(1)}, bf16[16,256]{1,0:T(8,128)(2,1)S(1)}, u32[]{:S(2)}, u32[]{:S(2)}) collective-permute-start(bf16[16,256]{1,0:T(8,128)(2,1)S(1)} %get-tuple-element.69.refs_1_), channel_id=1, source_target_pairs={{0,64},{1,65},{2,66},{3,67},{4,68},{5,69},{6,70},{7,71},{8,72},{9,... | collective-permute-start | bytes 24584 | tf_op jit(solution)/shard_map/ppermute | solution.py:791
  60.9 7.2 %collective-permute-start.13 = (bf16[128,512]{1,0:T(8,128)(2,1)S(1)}, bf16[128,512]{1,0:T(8,128)(2,1)S(1)}, u32[]{:S(2)}, u32[]{:S(2)}) collective-permute-start(bf16[128,512]{1,0:T(8,128)(2,1)S(1)} %get-tuple-element.85.refs_3_.refs_1_), channel_id=1, source_target_pairs={{0,16},{16,0},{32,48},{48,32},{64,80},{80,64},{96,112},{112,96},{1... | collective-permute-start | bytes 393224 | tf_op jit(solution)/shard_map/ppermute | solution.py:813
  61.0 7.1 %collective-permute-start.14 = (bf16[16,512]{1,0:T(8,128)(2,1)S(1)}, bf16[16,512]{1,0:T(8,128)(2,1)S(1)}, u32[]{:S(2)}, u32[]{:S(2)}) collective-permute-start(bf16[16,512]{1,0:T(8,128)(2,1)S(1)} %get-tuple-element.86.refs_0_), channel_id=1, source_target_pairs={{0,2},{1,3},{2,0},{3,1},{4,6},{5,7},{6,4},{7,5},{8,10},{9,11},{10,... | collective-permute-start | bytes 49160 | tf_op jit(solution)/shard_map/ppermute | solution.py:814
  62.1 6.0 %collective-permute-start.15 = (bf16[16,512]{1,0:T(8,128)(2,1)S(1)}, bf16[16,512]{1,0:T(8,128)(2,1)S(1)}, u32[]{:S(2)}, u32[]{:S(2)}) collective-permute-start(bf16[16,512]{1,0:T(8,128)(2,1)S(1)} %get-tuple-element.86.refs_0_), channel_id=1, source_target_pairs={{0,18},{1,19},{2,16},{3,17},{4,22},{5,23},{6,20},{7,21},{8,26},{9,... | collective-permute-start | bytes 49160 | tf_op jit(solution)/shard_map/ppermute | solution.py:815
  68.1 11.0 %collective-permute-start.16 = (bf16[128,512]{1,0:T(8,128)(2,1)S(1)}, bf16[128,512]{1,0:T(8,128)(2,1)S(1)}, u32[]{:S(2)}, u32[]{:S(2)}) collective-permute-start(bf16[128,512]{1,0:T(8,128)(2,1)S(1)} %get-tuple-element.88.refs_2_), channel_id=1, source_target_pairs={{0,32},{16,48},{32,64},{48,80},{64,96},{80,112},{96,0},{112,16},{1... | collective-permute-start | bytes 393224 | tf_op jit(solution)/shard_map/ppermute | solution.py:835
  68.3 10.8 %collective-permute-start.17 = (bf16[128,512]{1,0:T(8,128)(2,1)S(1)}, bf16[128,512]{1,0:T(8,128)(2,1)S(1)}, u32[]{:S(2)}, u32[]{:S(2)}) collective-permute-start(bf16[128,512]{1,0:T(8,128)(2,1)S(1)} %get-tuple-element.88.refs_2_), channel_id=1, source_target_pairs={{0,96},{16,112},{32,0},{48,16},{64,32},{80,48},{96,64},{112,80},{1... | collective-permute-start | bytes 393224 | tf_op jit(solution)/shard_map/ppermute | solution.py:836
  71.4 7.0 %collective-permute-start.18 = (bf16[64,512]{1,0:T(8,128)(2,1)S(1)}, bf16[64,512]{1,0:T(8,128)(2,1)S(1)}, u32[]{:S(2)}, u32[]{:S(2)}) collective-permute-start(bf16[64,512]{1,0:T(8,128)(2,1)S(1)} %get-tuple-element.89.refs_5_), channel_id=1, source_target_pairs={{0,4},{1,5},{2,6},{3,7},{4,8},{5,9},{6,10},{7,11},{8,12},{9,13},{1... | collective-permute-start | bytes 196616 | tf_op jit(solution)/shard_map/ppermute | solution.py:834
  72.7 5.8 %collective-permute-start.19 = (bf16[64,512]{1,0:T(8,128)(2,1)S(1)}, bf16[64,512]{1,0:T(8,128)(2,1)S(1)}, u32[]{:S(2)}, u32[]{:S(2)}) collective-permute-start(bf16[64,512]{1,0:T(8,128)(2,1)S(1)} %get-tuple-element.89.refs_5_), channel_id=1, source_target_pairs={{0,8},{1,9},{2,10},{3,11},{4,12},{5,13},{6,14},{7,15},{8,0},{9,1},... | collective-permute-start | bytes 196616 | tf_op jit(solution)/shard_map/ppermute | solution.py:834
  74.8 4.3 %collective-permute-start.20 = (bf16[64,512]{1,0:T(8,128)(2,1)S(1)}, bf16[64,512]{1,0:T(8,128)(2,1)S(1)}, u32[]{:S(2)}, u32[]{:S(2)}) collective-permute-start(bf16[64,512]{1,0:T(8,128)(2,1)S(1)} %get-tuple-element.89.refs_5_), channel_id=1, source_target_pairs={{0,12},{1,13},{2,14},{3,15},{4,0},{5,1},{6,2},{7,3},{8,4},{9,5},{1... | collective-permute-start | bytes 196616 | tf_op jit(solution)/shard_map/ppermute | solution.py:834
  79.7 16.9 %collective-permute-start.21 = (bf16[3,128,512]{2,1,0:T(8,128)(2,1)S(1)}, bf16[3,128,512]{2,1,0:T(8,128)(2,1)S(1)}, u32[]{:S(2)}, u32[]{:S(2)}) collective-permute-start(bf16[3,128,512]{2,1,0:T(8,128)(2,1)S(1)} %get-tuple-element.91.refs_2_), channel_id=1, source_target_pairs={{0,1},{1,2},{2,3},{3,4},{4,5},{5,6},{6,7},{7,8},{8,9},{9,10},{10,1... | collective-permute-start | bytes 1179656 | tf_op jit(solution)/shard_map/ppermute | solution.py:587
  79.8 15.4 %collective-permute-start.23 = (bf16[256,512]{1,0:T(8,128)(2,1)S(1)}, bf16[256,512]{1,0:T(8,128)(2,1)S(1)}, u32[]{:S(2)}, u32[]{:S(2)}) collective-permute-start(bf16[256,512]{1,0:T(8,128)(2,1)S(1)} %get-tuple-element.93.refs_3_), channel_id=1, source_target_pairs={{0,32},{16,48},{32,64},{48,80},{64,96},{80,112},{96,0},{112,16},{1... | collective-permute-start | bytes 786440 | tf_op jit(solution)/shard_map/ppermute | solution.py:845
  79.9 15.8 %collective-permute-start.24 = (bf16[256,512]{1,0:T(8,128)(2,1)S(1)}, bf16[256,512]{1,0:T(8,128)(2,1)S(1)}, u32[]{:S(2)}, u32[]{:S(2)}) collective-permute-start(bf16[256,512]{1,0:T(8,128)(2,1)S(1)} %get-tuple-element.93.refs_3_), channel_id=1, source_target_pairs={{0,64},{16,80},{32,96},{48,112},{64,0},{80,16},{96,32},{112,48},{1... | collective-permute-start | bytes 786440 | tf_op jit(solution)/shard_map/ppermute | solution.py:845
  81.3 15.1 %collective-permute-start.25 = (bf16[256,512]{1,0:T(8,128)(2,1)S(1)}, bf16[256,512]{1,0:T(8,128)(2,1)S(1)}, u32[]{:S(2)}, u32[]{:S(2)}) collective-permute-start(bf16[256,512]{1,0:T(8,128)(2,1)S(1)} %get-tuple-element.93.refs_3_), channel_id=1, source_target_pairs={{0,96},{16,112},{32,0},{48,16},{64,32},{80,48},{96,64},{112,80},{1... | collective-permute-start | bytes 786440 | tf_op jit(solution)/shard_map/ppermute | solution.py:845
  83.1 13.8 %collective-permute-start.22 = (bf16[3,128,512]{2,1,0:T(8,128)(2,1)S(1)}, bf16[3,128,512]{2,1,0:T(8,128)(2,1)S(1)}, u32[]{:S(2)}, u32[]{:S(2)}) collective-permute-start(bf16[3,128,512]{2,1,0:T(8,128)(2,1)S(1)} %get-tuple-element.91.refs_2_), channel_id=1, source_target_pairs={{0,15},{1,0},{2,1},{3,2},{4,3},{5,4},{6,5},{7,6},{8,7},{9,8},{10,9... | collective-permute-start | bytes 1179656 | tf_op jit(solution)/shard_map/ppermute | solution.py:587
  101.3 9.2 %collective-permute-start.32 = (bf16[128,512]{1,0:T(8,128)(2,1)S(1)}, bf16[128,512]{1,0:T(8,128)(2,1)S(1)}, u32[]{:S(2)}, u32[]{:S(2)}) collective-permute-start(bf16[128,512]{1,0:T(8,128)(2,1)S(1)} %mesh.1.refs_3_.refs_2_), channel_id=1, source_target_pairs={{0,16},{16,0},{32,48},{48,32},{64,80},{80,64},{96,112},{112,96},{1... | collective-permute-start | bytes 393224 | tf_op jit(solution)/shard_map/ppermute | solution.py:594
  102.7 10.7 %collective-permute-start.33 = (bf16[128,512]{1,0:T(8,128)(2,1)S(1)}, bf16[128,512]{1,0:T(8,128)(2,1)S(1)}, u32[]{:S(2)}, u32[]{:S(2)}) collective-permute-start(bf16[128,512]{1,0:T(8,128)(2,1)S(1)} %mesh.1.refs_3_.refs_2_), channel_id=1, source_target_pairs={{16,32},{48,64},{80,96},{32,16},{64,48},{96,80},{17,33},{49,65},{8... | collective-permute-start | bytes 393224 | tf_op jit(solution)/shard_map/ppermute | solution.py:593
  106.5 11.3 %collective-permute-start.30 = (bf16[128,512]{1,0:T(8,128)(2,1)S(1)}, bf16[128,512]{1,0:T(8,128)(2,1)S(1)}, u32[]{:S(2)}, u32[]{:S(2)}) collective-permute-start(bf16[128,512]{1,0:T(8,128)(2,1)S(1)} %mesh.1.refs_3_.refs_2_), channel_id=1, source_target_pairs={{0,1},{1,2},{2,3},{3,4},{4,5},{5,6},{6,7},{7,8},{8,9},{9,10},{10,1... | collective-permute-start | bytes 393224 | tf_op jit(solution)/shard_map/ppermute | solution.py:587
  106.6 11.3 %collective-permute-start.31 = (bf16[128,512]{1,0:T(8,128)(2,1)S(1)}, bf16[128,512]{1,0:T(8,128)(2,1)S(1)}, u32[]{:S(2)}, u32[]{:S(2)}) collective-permute-start(bf16[128,512]{1,0:T(8,128)(2,1)S(1)} %mesh.1.refs_3_.refs_2_), channel_id=1, source_target_pairs={{0,15},{1,0},{2,1},{3,2},{4,3},{5,4},{6,5},{7,6},{8,7},{9,8},{10,9... | collective-permute-start | bytes 393224 | tf_op jit(solution)/shard_map/ppermute | solution.py:587
  113.9 8.5 %collective-permute-start.34 = (bf16[2,128,512]{2,1,0:T(8,128)(2,1)S(1)}, bf16[2,128,512]{2,1,0:T(8,128)(2,1)S(1)}, u32[]{:S(2)}, u32[]{:S(2)}) collective-permute-start(bf16[2,128,512]{2,1,0:T(8,128)(2,1)S(1)} %pair.3.refs_4_), channel_id=1, source_target_pairs={{0,1},{1,2},{2,3},{3,4},{4,5},{5,6},{6,7},{7,8},{8,9},{9,10},{10,1... | collective-permute-start | bytes 786440 | tf_op jit(solution)/shard_map/ppermute | solution.py:587
  114.0 8.4 %collective-permute-start.35 = (bf16[2,128,512]{2,1,0:T(8,128)(2,1)S(1)}, bf16[2,128,512]{2,1,0:T(8,128)(2,1)S(1)}, u32[]{:S(2)}, u32[]{:S(2)}) collective-permute-start(bf16[2,128,512]{2,1,0:T(8,128)(2,1)S(1)} %pair.3.refs_4_), channel_id=1, source_target_pairs={{0,15},{1,0},{2,1},{3,2},{4,3},{5,4},{6,5},{7,6},{8,7},{9,8},{10,9... | collective-permute-start | bytes 786440 | tf_op jit(solution)/shard_map/ppermute | solution.py:587
  (5 other events, 15.5 us)

commit v2 on v1

--- a/solution.py
+++ b/solution.py
@@ -307,7 +307,6 @@
     masks, ranks, q, edges, sums = refs
     band = lax.shift_right_logical(place[0, 4], 4)
     lists = tuple(zip(sources, buckets, outs))
-    q[...] = jnp.zeros_like(q)
 
     def listed(src, c):
         return src[MESH_NODES:LISTED, :].astype(F32)[8 * c : 8 * (c + 1), :]
@@ -360,6 +359,9 @@
 
     @pl.when(total > 0)
     def _():
+        for bucket in sorted(set(range(9)) - set(buckets)):
+            q[MESH_NODES * bucket : MESH_NODES * (bucket + 1), :] = jnp.zeros((MESH_NODES, WIDTH), BF)
+            sums[MESH_NODES * bucket : MESH_NODES * (bucket + 1), :] = jnp.zeros((MESH_NODES, WIDTH), F32)
         across = lax.broadcasted_iota(I32, (n, 1), 0) // CHUNKS
         base = jnp.zeros((n, 1), F32)
         for i in range(len(lists) - 1):
@@ -525,17 +527,18 @@
 
 def mesh_body(
     count, fine, edges, a0, a1, a2, a3, b0, b1, b2, b3, recv, mesh_one, w_geom, folded, first_node, second, w_send,
-    send, rows, total,
+    send, total,
 ):
     parts = (a0, a1, a2, a3, b0, b1, b2, b3)
     n = a0.shape[0]
-    for k, part in enumerate(parts):
-        rows[n * k : n * (k + 1), :] = part[...]
     q = recv[0:COARSE_DEV, :]
 
     def hidden_sum(d):
         pick = one_hot(d[:, 1:2].astype(I32), MESH_NODES)
-        pre = mm(one_hot(d[:, 0:1].astype(I32), len(parts) * n), rows[...])
+        spread = one_hot(d[:, 0:1].astype(I32), len(parts) * n)
+        pre = mm(spread[:, 0:n], parts[0][...])
+        for k in range(1, len(parts)):
+            pre += mm(spread[:, n * k : n * (k + 1)], parts[k][...])
         pre += mm(pick[:, 0:COARSE_DEV], q) + mm(d.astype(BF), w_geom[...])
         return mm_t(pick, silu(pre).astype(BF))
 
@@ -859,7 +862,7 @@
         shaped(mesh_rows, BF),
         [SMEM] + [V] * 12 + [geom_of(1)] + [V] * 4,
         (c_count, fine, c_edges, *quarter, *swapped, proc_recv, mesh_one, geom, folded[1], *kept[4:7]),
-        [pltpu.VMEM((128 * COARSE_DEV, WIDTH), BF), pltpu.VMEM(mesh_rows, F32)],
+        [pltpu.VMEM(mesh_rows, F32)],
         flops=4 * grid_flops,
         moved=6 << 20,
         name="mesh",

time: 129 us -> 129 us (level)
  no operation moved by 1% of the time
where the time goes in v2:
time: 129 us; the launch traced here: 127 us
  starting transfers between devices  59.8 us (46%)
  Pallas kernels  47.5 us (37%)
  waiting for transfers between devices  18.6 us (14%)
    pallas_call x22, Pallas kernels, kernel_call(): pl.pallas_call(run, out_shape=outs, in_specs=[HBM if isinstance(q, Load)...  47.5 us
    ppermute x14, starting transfers between devices, shift(): return lax.ppermute(value, axis, pairs)  24.7 us
    ppermute x3, starting transfers between devices, swap_bands(): second = lax.ppermute(second, 'lat', later)  10.8 us
    ppermute x3, waiting for transfers between devices, per_device(): lax.ppermute(rows, 'lat', along_z(s))  9.58 us
    ppermute x3, starting transfers between devices, swap_bands(): return (lax.ppermute(first, 'lat', [(i, i ^ 1) for i in range(8)]), second)  6.17 us
    ppermute x3, starting transfers between devices, per_device(): lax.ppermute(beside, 'lon', along_y(s))  5.3 us
    ppermute x3, waiting for transfers between devices, swap_bands(): second = lax.ppermute(second, 'lat', later)  4.38 us
    ppermute x3, starting transfers between devices, per_device(): lax.ppermute(rows, 'lat', along_z(s))  3.3 us
  transfers between devices with their start and end apart: 36, of which 10 were waited for; matrix products, arithmetic and copies ran while one was open for 0% of the time, Pallas kernels for 25%

profile of v2, /device:TPU:4, one launch (start us, length us, event | category | flops | bytes accessed | tf_op | source)
XLA Modules:
  0.0 127.0 jit_solution(16253914940010288009)
XLA Ops:
  1.8 3.8 %collective-permute-start.1 = (bf16[176,512]{1,0:T(8,128)(2,1)S(1)}, bf16[176,512]{1,0:T(8,128)(2,1)S(1)}, u32[]{:S(2)}, u32[]{:S(2)}) collective-permute-start(bf16[176,512]{1,0:T(8,128)(2,1)S(1)} %get-tuple-element.53), channel_id=1, source_target_pairs={{0,15},{1,0},{2,1},{3,2},{4,3},{5,4},{6,5},{7,6},{8,7},{9,8},{10,9... | collective-permute-start | bytes 540680 | tf_op jit(solution)/shard_map/ppermute | solution.py:590
  6.0 4.5 %collective-permute-start.3 = (bf16[176,512]{1,0:T(8,128)(2,1)S(1)}, bf16[176,512]{1,0:T(8,128)(2,1)S(1)}, u32[]{:S(2)}, u32[]{:S(2)}) collective-permute-start(bf16[176,512]{1,0:T(8,128)(2,1)S(1)} %get-tuple-element.53), channel_id=1, source_target_pairs={{16,32},{48,64},{80,96},{112,0},{32,16},{64,48},{96,80},{0,112},{1... | collective-permute-start | bytes 540680 | tf_op jit(solution)/shard_map/ppermute | solution.py:596
  10.5 3.9 %embed.1 = (bf16[1024,512]{1,0:T(8,128)(2,1)S(1)}, bf16[512,512]{1,0:T(8,128)(2,1)S(1)}) custom-call(bf16[1,1,474,1024]{3,2,1,0:T(8,128)(2,1)} %bitcast.19, bf16[474,512]{1,0:T(8,128)(2,1)} %refs_1_.6, bf16[512,512]{1,0:T(8,128)(2,1)} %refs_2_.6, bf16[3,3,512,512]{3,2,1,0:T(8,128)(2,1)} %refs_1_.9), custom_call_target="tpu_custom_call" | custom-call | flops 1073741824 | bytes 4194304 | tf_op jit(solution)/shard_map/embed/pallas_call | solution.py:135
  15.5 2.9 %own_first.1 = (f32[128,512]{1,0:T(8,128)S(1)}, bf16[32,512]{1,0:T(8,128)(2,1)S(1)}) custom-call(bf16[1,1,128,512]{3,2,1,0:T(8,128)(2,1)} %refs_5_.5, bf16[64,512]{1,0:T(8,128)(2,1)S(1)} %get-tuple-element.54.refs_1_, bf16[1024,512]{1,0:T(8,128)(2,1)S(1)} %send.1.refs_2_.refs_5_.refs_8_, bf16[3,3,512,512]{3,2,1,0:T(8,128)(2,1)} %refs_1_.9, ...), custom_call_target="tpu_custom_call" | custom-call | flops 1073741824 | bytes 3145728 | tf_op jit(solution)/shard_map/own_first/pallas_call | solution.py:135
  19.1 3.8 %collective-permute-start.5 = (bf16[2,176,512]{2,1,0:T(8,128)(2,1)S(1)}, bf16[2,176,512]{2,1,0:T(8,128)(2,1)S(1)}, u32[]{:S(2)}, u32[]{:S(2)}) collective-permute-start(bf16[2,176,512]{2,1,0:T(8,128)(2,1)S(1)} %pair.2.refs_3_.refs_4_), channel_id=1, source_target_pairs={{0,15},{1,0},{2,1},{3,2},{4,3},{5,4},{6,5},{7,6},{8,7},{9,8},{10,9... | collective-permute-start | bytes 1081352 | tf_op jit(solution)/shard_map/ppermute | solution.py:590
  22.9 3.0 %own_last.1.refs_6_.refs_0_ = f32[128,512]{1,0:T(8,128)S(1)} custom-call(bf16[1,1,128,512]{3,2,1,0:T(8,128)(2,1)} %refs_5_.5, bf16[32,512]{1,0:T(8,128)(2,1)S(1)} %get-tuple-element.62.refs_1_, bf16[1024,512]{1,0:T(8,128)(2,1)S(1)} %send.1.refs_2_.refs_5_.refs_8_, bf16[3,3,512,512]{3,2,1,0:T(8,128)(2,1)} %refs_1_.9, ...), custom_call_target="tpu_custom_call" | custom-call | flops 1073741824 | bytes 3145728 | tf_op jit(solution)/shard_map/own_last/pallas_call | solution.py:135
  25.9 4.3 %beside.1 = (bf16[128,512]{1,0:T(8,128)(2,1)S(1)}, bf16[128,512]{1,0:T(8,128)(2,1)S(1)}, bf16[128,512]{1,0:T(8,128)(2,1)S(1)}, bf16[128,512]{1,0:T(8,128)(2,1)S(1)}, bf16[16,256]{1,0:T(8,128)(2,1)S(1)}) custom-call(s32[1,5]{1,0:T(1,128)S(1)} %bitcast.13, bf16[176,512]{1,0:T(8,128)(2,1)S(1)} %collective-permute-done.refs_2_.refs_1_, ...), custom_call_target="tpu_custom_call" | custom-call | flops 1073741824 | bytes 5242880 | tf_op jit(solution)/shard_map/beside/pallas_call | solution.py:135
  31.0 4.1 %corners.1 = (bf16[128,512]{1,0:T(8,128)(2,1)S(1)}, bf16[128,512]{1,0:T(8,128)(2,1)S(1)}, bf16[128,512]{1,0:T(8,128)(2,1)S(1)}, bf16[128,512]{1,0:T(8,128)(2,1)S(1)}, bf16[16,256]{1,0:T(8,128)(2,1)S(1)}) custom-call(s32[1,5]{1,0:T(1,128)S(1)} %bitcast.14, bf16[2,176,512]{2,1,0:T(8,128)(2,1)S(1)} %collective-permute-done.4.refs_1_.refs_2_, ...), custom_call_target="tpu_custom_call" | custom-call | flops 1073741824 | bytes 5242880 | tf_op jit(solution)/shard_map/corners/pallas_call | solution.py:135
  35.2 1.8 %collective-permute-start.10 = (bf16[2,128,512]{2,1,0:T(8,128)(2,1)S(1)}, bf16[2,128,512]{2,1,0:T(8,128)(2,1)S(1)}, u32[]{:S(2)}, u32[]{:S(2)}) collective-permute-start(bf16[2,128,512]{2,1,0:T(8,128)(2,1)S(1)} %get-tuple-element.67.refs_6_), channel_id=1, source_target_pairs={{0,15},{1,0},{2,1},{3,2},{4,3},{5,4},{6,5},{7,6},{8,7},{9,8},{10,9... | collective-permute-start | bytes 786440 | tf_op jit(solution)/shard_map/ppermute | solution.py:590
  37.0 2.5 %prep.1 = (f32[6,128,16]{2,1,0:T(8,128)S(1)}, f32[3,1024,16]{2,1,0:T(8,128)S(1)}, bf16[128,512]{1,0:T(8,128)(2,1)S(1)}, bf16[128,512]{1,0:T(8,128)(2,1)S(1)}, bf...) custom-call(s32[1,1,768]{2,1,0:T(1,128)} %refs_0_.7, ...), custom_call_target="tpu_custom_call" | custom-call | flops 536870912 | tf_op jit(solution)/shard_map/prep/pallas_call | solution.py:135
  39.6 3.9 %collective-permute-start.8 = (bf16[128,512]{1,0:T(8,128)(2,1)S(1)}, bf16[128,512]{1,0:T(8,128)(2,1)S(1)}, u32[]{:S(2)}, u32[]{:S(2)}) collective-permute-start(bf16[128,512]{1,0:T(8,128)(2,1)S(1)} %get-tuple-element.74), channel_id=1, source_target_pairs={{0,15},{1,0},{2,1},{3,2},{4,3},{5,4},{6,5},{7,6},{8,7},{9,8},{10,9... | collective-permute-start | bytes 393224 | tf_op jit(solution)/shard_map/ppermute | solution.py:590
  45.6 4.3 %collective-permute-start.11 = (bf16[128,512]{1,0:T(8,128)(2,1)S(1)}, bf16[128,512]{1,0:T(8,128)(2,1)S(1)}, u32[]{:S(2)}, u32[]{:S(2)}) collective-permute-start(bf16[128,512]{1,0:T(8,128)(2,1)S(1)} %get-tuple-element.78.refs_6_), channel_id=1, source_target_pairs={{0,16},{16,0},{32,48},{48,32},{64,80},{80,64},{96,112},{112,96},{1... | collective-permute-start | bytes 393224 | tf_op jit(solution)/shard_map/ppermute | solution.py:597
  49.9 2.5 %collective-permute-start.12 = (bf16[128,512]{1,0:T(8,128)(2,1)S(1)}, bf16[128,512]{1,0:T(8,128)(2,1)S(1)}, u32[]{:S(2)}, u32[]{:S(2)}) collective-permute-start(bf16[128,512]{1,0:T(8,128)(2,1)S(1)} %get-tuple-element.79), channel_id=1, source_target_pairs={{16,32},{48,64},{80,96},{32,16},{64,48},{96,80},{17,33},{49,65},{8... | collective-permute-start | bytes 393224 | tf_op jit(solution)/shard_map/ppermute | solution.py:596
  53.4 2.6 %fold.1 = (bf16[512,512]{1,0:T(8,128)(2,1)S(1)}, bf16[512,512]{1,0:T(8,128)(2,1)S(1)}, bf16[512,512]{1,0:T(8,128)(2,1)S(1)}) custom-call(bf16[3,3,512,512]{3,2,1,0:T(8,128)(2,1)} %refs_1_.9, bf16[3,1024,512]{2,1,0:T(8,128)(2,1)} %refs_2_.9, bf16[3,3,512,512]{3,2,1,0:T(8,128)(2,1)} %refs_1_.9, bf16[3,1024,512]{2,1,0:T(8,128)(2,1)} %refs_2_.9, ...), custom_call_target="tpu_custom_call" | custom-call | flops 805306368 | bytes 4194304 | tf_op jit(solution)/shard_map/fold/pallas_call | solution.py:135
  59.1 1.7 %node.1 = (bf16[128,512]{1,0:T(8,128)(2,1)S(1)}, bf16[128,512]{1,0:T(8,128)(2,1)S(1)}, bf16[128,512]{1,0:T(8,128)(2,1)S(1)}, bf16[16,512]{1,0:T(8,128)(2,1)S(1)}) custom-call(f32[128,512]{1,0:T(8,128)S(1)} %own_last.1.refs_6_.refs_0_, bf16[128,512]{1,0:T(8,128)(2,1)S(1)} %collective-permute-done.7.refs_1_, ...), custom_call_target="tpu_custom_call" | custom-call | flops 469762048 | bytes 4194304 | tf_op jit(solution)/shard_map/node/pallas_call | solution.py:135
  62.0 3.0 %collective-permute-start.15 = (bf16[16,512]{1,0:T(8,128)(2,1)S(1)}, bf16[16,512]{1,0:T(8,128)(2,1)S(1)}, u32[]{:S(2)}, u32[]{:S(2)}) collective-permute-start(bf16[16,512]{1,0:T(8,128)(2,1)S(1)} %get-tuple-element.86.refs_0_), channel_id=1, source_target_pairs={{0,18},{1,19},{2,16},{3,17},{4,22},{5,23},{6,20},{7,21},{8,26},{9,... | collective-permute-start | bytes 49160 | tf_op jit(solution)/shard_map/ppermute | solution.py:818
  65.0 3.0 %grid.1 = (bf16[1024,512]{1,0:T(8,128)(2,1)S(1)}, f32[1024,512]{1,0:T(8,128)S(1)}) custom-call(bf16[1024,512]{1,0:T(8,128)(2,1)S(1)} %get-tuple-element.55.refs_0_, bf16[3,3,512,512]{3,2,1,0:T(8,128)(2,1)} %refs_1_.9, bf16[3,1024,512]{2,1,0:T(8,128)(2,1)} %refs_2_.9, bf16[128,512]{1,0:T(8,128)(2,1)S(1)} %get-tuple-element.85.refs_3_.refs_1_), custom_call_target="tpu_custom_call" | custom-call | flops 1073741824 | bytes 5242880 | tf_op jit(solution)/shard_map/grid/pallas_call | solution.py:135
  68.3 3.1 %collective-permute-start.17 = (bf16[128,512]{1,0:T(8,128)(2,1)S(1)}, bf16[128,512]{1,0:T(8,128)(2,1)S(1)}, u32[]{:S(2)}, u32[]{:S(2)}) collective-permute-start(bf16[128,512]{1,0:T(8,128)(2,1)S(1)} %get-tuple-element.88.refs_2_), channel_id=1, source_target_pairs={{0,96},{16,112},{32,0},{48,16},{64,32},{80,48},{96,64},{112,80},{1... | collective-permute-start | bytes 393224 | tf_op jit(solution)/shard_map/ppermute | solution.py:839
  72.7 2.1 %collective-permute-start.19 = (bf16[64,512]{1,0:T(8,128)(2,1)S(1)}, bf16[64,512]{1,0:T(8,128)(2,1)S(1)}, u32[]{:S(2)}, u32[]{:S(2)}) collective-permute-start(bf16[64,512]{1,0:T(8,128)(2,1)S(1)} %get-tuple-element.89.refs_5_), channel_id=1, source_target_pairs={{0,8},{1,9},{2,10},{3,11},{4,12},{5,13},{6,14},{7,15},{8,0},{9,1},... | collective-permute-start | bytes 196616 | tf_op jit(solution)/shard_map/ppermute | solution.py:837
  74.8 1.9 %collective-permute-start.20 = (bf16[64,512]{1,0:T(8,128)(2,1)S(1)}, bf16[64,512]{1,0:T(8,128)(2,1)S(1)}, u32[]{:S(2)}, u32[]{:S(2)}) collective-permute-start(bf16[64,512]{1,0:T(8,128)(2,1)S(1)} %get-tuple-element.89.refs_5_), channel_id=1, source_target_pairs={{0,12},{1,13},{2,14},{3,15},{4,0},{5,1},{6,2},{7,3},{8,4},{9,5},{1... | collective-permute-start | bytes 196616 | tf_op jit(solution)/shard_map/ppermute | solution.py:837
  76.6 1.7 %coarse_edges.1 = (f32[768,16]{1,0:T(8,128)S(1)}, s32[1,1]{1,0:T(1,128)}) custom-call(s32[1,5]{1,0:T(1,128)S(1)} %bitcast.16, bf16[16,256]{1,0:T(8,128)(2,1)S(1)} %get-tuple-element.69.refs_1_, bf16[16,256]{1,0:T(8,128)(2,1)S(1)} %get-tuple-element.70.refs_2_, bf16[16,256]{1,0:T(8,128)(2,1)S(1)} %collective-permute-done.6.refs_3_.refs_11_), custom_call_target="tpu_custom_call" | custom-call | flops 67108864 | tf_op jit(solution)/shard_map/coarse_edges/pallas_call | solution.py:135
  81.3 1.8 %collective-permute-start.25 = (bf16[256,512]{1,0:T(8,128)(2,1)S(1)}, bf16[256,512]{1,0:T(8,128)(2,1)S(1)}, u32[]{:S(2)}, u32[]{:S(2)}) collective-permute-start(bf16[256,512]{1,0:T(8,128)(2,1)S(1)} %get-tuple-element.93.refs_3_), channel_id=1, source_target_pairs={{0,96},{16,112},{32,0},{48,16},{64,32},{80,48},{96,64},{112,80},{1... | collective-permute-start | bytes 786440 | tf_op jit(solution)/shard_map/ppermute | solution.py:848
  83.0 3.2 %collective-permute-start.22 = (bf16[3,128,512]{2,1,0:T(8,128)(2,1)S(1)}, bf16[3,128,512]{2,1,0:T(8,128)(2,1)S(1)}, u32[]{:S(2)}, u32[]{:S(2)}) collective-permute-start(bf16[3,128,512]{2,1,0:T(8,128)(2,1)S(1)} %get-tuple-element.91.refs_2_), channel_id=1, source_target_pairs={{0,15},{1,0},{2,1},{3,2},{4,3},{5,4},{6,5},{7,6},{8,7},{9,8},{10,9... | collective-permute-start | bytes 1179656 | tf_op jit(solution)/shard_map/ppermute | solution.py:590
  86.2 8.9 %collective-permute-done.23.refs_6_.refs_4_ = bf16[256,512]{1,0:T(8,128)(2,1)S(1)} collective-permute-done((bf16[256,512]{1,0:T(8,128)(2,1)S(1)}, bf16[256,512]{1,0:T(8,128)(2,1)S(1)}, u32[]{:S(2)}, u32[]{:S(2)}) %collective-permute-start.23) | collective-permute-done | bytes 262176 | tf_op jit(solution)/shard_map/ppermute | solution.py:848
  96.9 1.7 %fine.1.refs_1_ = f32[128,512]{1,0:T(8,128)S(1)} custom-call(f32[6,128,16]{2,1,0:T(8,128)S(1)} %get-tuple-element.72.refs_5_.refs_0_, bf16[3,128,512]{2,1,0:T(8,128)(2,1)S(1)} %collective-permute-done.21.refs_1_, bf16[3,128,512]{2,1,0:T(8,128)(2,1)S(1)} %get-tuple-element.91.refs_2_, bf16[3,128,512]{2,1,0:T(8,128)(2,1)S(1)} %collective-permute-done.22.refs_3_, ...), custom_call_target="tpu_custom_call" | custom-call | flops 1073741824 | bytes 3145728 | tf_op jit(solution)/shard_map/fine/pallas_call | solution.py:135
  98.7 2.6 %mesh.1.refs_3_.refs_2_ = bf16[128,512]{1,0:T(8,128)(2,1)S(1)} custom-call(s32[1,1]{1,0:T(1,128)} %get-tuple-element.71.refs_0_, f32[128,512]{1,0:T(8,128)S(1)} %fine.1.refs_1_, f32[768,16]{1,0:T(8,128)S(1)} %get-tuple-element.90.refs_9_.refs_7_.refs_2_, bf16[256,512]{1,0:T(8,128)(2,1)S(1)} %get-tuple-element.93.refs_3_, ...), custom_call_target="tpu_custom_call" | custom-call | flops 2147483648 | bytes 6291456 | tf_op jit(solution)/shard_map/mesh/pallas_call | solution.py:135
  102.7 3.8 %collective-permute-start.33 = (bf16[128,512]{1,0:T(8,128)(2,1)S(1)}, bf16[128,512]{1,0:T(8,128)(2,1)S(1)}, u32[]{:S(2)}, u32[]{:S(2)}) collective-permute-start(bf16[128,512]{1,0:T(8,128)(2,1)S(1)} %mesh.1.refs_3_.refs_2_), channel_id=1, source_target_pairs={{16,32},{48,64},{80,96},{32,16},{64,48},{96,80},{17,33},{49,65},{8... | collective-permute-start | bytes 393224 | tf_op jit(solution)/shard_map/ppermute | solution.py:596
  106.6 3.8 %collective-permute-start.31 = (bf16[128,512]{1,0:T(8,128)(2,1)S(1)}, bf16[128,512]{1,0:T(8,128)(2,1)S(1)}, u32[]{:S(2)}, u32[]{:S(2)}) collective-permute-start(bf16[128,512]{1,0:T(8,128)(2,1)S(1)} %mesh.1.refs_3_.refs_2_), channel_id=1, source_target_pairs={{0,15},{1,0},{2,1},{3,2},{4,3},{5,4},{6,5},{7,6},{8,7},{9,8},{10,9... | collective-permute-start | bytes 393224 | tf_op jit(solution)/shard_map/ppermute | solution.py:590
  110.5 2.9 %collective-permute-done.33.refs_2_ = bf16[128,512]{1,0:T(8,128)(2,1)S(1)} collective-permute-done((bf16[128,512]{1,0:T(8,128)(2,1)S(1)}, bf16[128,512]{1,0:T(8,128)(2,1)S(1)}, u32[]{:S(2)}, u32[]{:S(2)}) %collective-permute-start.33) | collective-permute-done | bytes 131104 | tf_op jit(solution)/shard_map/ppermute | solution.py:596
  114.0 3.8 %collective-permute-start.35 = (bf16[2,128,512]{2,1,0:T(8,128)(2,1)S(1)}, bf16[2,128,512]{2,1,0:T(8,128)(2,1)S(1)}, u32[]{:S(2)}, u32[]{:S(2)}) collective-permute-start(bf16[2,128,512]{2,1,0:T(8,128)(2,1)S(1)} %pair.3.refs_4_), channel_id=1, source_target_pairs={{0,15},{1,0},{2,1},{3,2},{4,3},{5,4},{6,5},{7,6},{8,7},{9,8},{10,9... | collective-permute-start | bytes 786440 | tf_op jit(solution)/shard_map/ppermute | solution.py:590
  117.9 4.5 %early.1.refs_1_ = f32[3,1024,512]{2,1,0:T(8,128)S(1)} custom-call(f32[3,1024,16]{2,1,0:T(8,128)S(1)} %get-tuple-element.68.refs_0_, bf16[128,512]{1,0:T(8,128)(2,1)S(1)} %collective-permute-done.30.refs_1_, bf16[128,512]{1,0:T(8,128)(2,1)S(1)} %mesh.1.refs_3_.refs_2_, bf16[128,512]{1,0:T(8,128)(2,1)S(1)} %collective-permute-done.31.refs_3_, ...), custom_call_target="tpu_custom_call" | custom-call | flops 2147483648 | bytes 8388608 | tf_op jit(solution)/shard_map/early/pallas_call | solution.py:135
  122.4 4.6 %decode.1 = bf16[227,1024]{1,0:T(8,128)(2,1)} custom-call(f32[3,1024,16]{2,1,0:T(8,128)S(1)} %get-tuple-element.68.refs_0_, f32[3,1024,512]{2,1,0:T(8,128)S(1)} %early.1.refs_1_, bf16[2,128,512]{2,1,0:T(8,128)(2,1)S(1)} %collective-permute-done.34.refs_2_, bf16[2,128,512]{2,1,0:T(8,128)(2,1)S(1)} %collective-permute-done.35.refs_3_, ...), custom_call_target="tpu_custom_call" | custom-call | flops 2684354560 | bytes 8388608 | tf_op jit(solution)/shard_map/decode/pallas_call | solution.py:135
  (65 shorter events, 19.8 us)
Async XLA Ops:
  1.7 12.9 %collective-permute-start = (bf16[176,512]{1,0:T(8,128)(2,1)S(1)}, bf16[176,512]{1,0:T(8,128)(2,1)S(1)}, u32[]{:S(2)}, u32[]{:S(2)}) collective-permute-start(bf16[176,512]{1,0:T(8,128)(2,1)S(1)} %get-tuple-element.53), channel_id=1, source_target_pairs={{0,1},{1,2},{2,3},{3,4},{4,5},{5,6},{6,7},{7,8},{8,9},{9,10},{10,1... | collective-permute-start | bytes 540680 | tf_op jit(solution)/shard_map/ppermute | solution.py:590
  1.8 12.8 %collective-permute-start.1 = (bf16[176,512]{1,0:T(8,128)(2,1)S(1)}, bf16[176,512]{1,0:T(8,128)(2,1)S(1)}, u32[]{:S(2)}, u32[]{:S(2)}) collective-permute-start(bf16[176,512]{1,0:T(8,128)(2,1)S(1)} %get-tuple-element.53), channel_id=1, source_target_pairs={{0,15},{1,0},{2,1},{3,2},{4,3},{5,4},{6,5},{7,6},{8,7},{9,8},{10,9... | collective-permute-start | bytes 540680 | tf_op jit(solution)/shard_map/ppermute | solution.py:590
  5.6 12.8 %collective-permute-start.2 = (bf16[176,512]{1,0:T(8,128)(2,1)S(1)}, bf16[176,512]{1,0:T(8,128)(2,1)S(1)}, u32[]{:S(2)}, u32[]{:S(2)}) collective-permute-start(bf16[176,512]{1,0:T(8,128)(2,1)S(1)} %get-tuple-element.53), channel_id=1, source_target_pairs={{0,16},{16,0},{32,48},{48,32},{64,80},{80,64},{96,112},{112,96},{1... | collective-permute-start | bytes 540680 | tf_op jit(solution)/shard_map/ppermute | solution.py:597
  6.0 12.4 %collective-permute-start.3 = (bf16[176,512]{1,0:T(8,128)(2,1)S(1)}, bf16[176,512]{1,0:T(8,128)(2,1)S(1)}, u32[]{:S(2)}, u32[]{:S(2)}) collective-permute-start(bf16[176,512]{1,0:T(8,128)(2,1)S(1)} %get-tuple-element.53), channel_id=1, source_target_pairs={{16,32},{48,64},{80,96},{112,0},{32,16},{64,48},{96,80},{0,112},{1... | collective-permute-start | bytes 540680 | tf_op jit(solution)/shard_map/ppermute | solution.py:596
  19.0 12.0 %collective-permute-start.4 = (bf16[2,176,512]{2,1,0:T(8,128)(2,1)S(1)}, bf16[2,176,512]{2,1,0:T(8,128)(2,1)S(1)}, u32[]{:S(2)}, u32[]{:S(2)}) collective-permute-start(bf16[2,176,512]{2,1,0:T(8,128)(2,1)S(1)} %pair.2.refs_3_.refs_4_), channel_id=1, source_target_pairs={{0,1},{1,2},{2,3},{3,4},{4,5},{5,6},{6,7},{7,8},{8,9},{9,10},{10,1... | collective-permute-start | bytes 1081352 | tf_op jit(solution)/shard_map/ppermute | solution.py:590
  19.1 11.9 %collective-permute-start.5 = (bf16[2,176,512]{2,1,0:T(8,128)(2,1)S(1)}, bf16[2,176,512]{2,1,0:T(8,128)(2,1)S(1)}, u32[]{:S(2)}, u32[]{:S(2)}) collective-permute-start(bf16[2,176,512]{2,1,0:T(8,128)(2,1)S(1)} %pair.2.refs_3_.refs_4_), channel_id=1, source_target_pairs={{0,15},{1,0},{2,1},{3,2},{4,3},{5,4},{6,5},{7,6},{8,7},{9,8},{10,9... | collective-permute-start | bytes 1081352 | tf_op jit(solution)/shard_map/ppermute | solution.py:590
  35.2 8.4 %collective-permute-start.10 = (bf16[2,128,512]{2,1,0:T(8,128)(2,1)S(1)}, bf16[2,128,512]{2,1,0:T(8,128)(2,1)S(1)}, u32[]{:S(2)}, u32[]{:S(2)}) collective-permute-start(bf16[2,128,512]{2,1,0:T(8,128)(2,1)S(1)} %get-tuple-element.67.refs_6_), channel_id=1, source_target_pairs={{0,15},{1,0},{2,1},{3,2},{4,3},{5,4},{6,5},{7,6},{8,7},{9,8},{10,9... | collective-permute-start | bytes 786440 | tf_op jit(solution)/shard_map/ppermute | solution.py:590
  37.0 7.9 %collective-permute-start.9 = (bf16[2,128,512]{2,1,0:T(8,128)(2,1)S(1)}, bf16[2,128,512]{2,1,0:T(8,128)(2,1)S(1)}, u32[]{:S(2)}, u32[]{:S(2)}) collective-permute-start(bf16[2,128,512]{2,1,0:T(8,128)(2,1)S(1)} %get-tuple-element.77), channel_id=1, source_target_pairs={{0,1},{1,2},{2,3},{3,4},{4,5},{5,6},{6,7},{7,8},{8,9},{9,10},{10,1... | collective-permute-start | bytes 786440 | tf_op jit(solution)/shard_map/ppermute | solution.py:590
  39.5 18.1 %collective-permute-start.7 = (bf16[128,512]{1,0:T(8,128)(2,1)S(1)}, bf16[128,512]{1,0:T(8,128)(2,1)S(1)}, u32[]{:S(2)}, u32[]{:S(2)}) collective-permute-start(bf16[128,512]{1,0:T(8,128)(2,1)S(1)} %get-tuple-element.73), channel_id=1, source_target_pairs={{0,1},{1,2},{2,3},{3,4},{4,5},{5,6},{6,7},{7,8},{8,9},{9,10},{10,1... | collective-permute-start | bytes 393224 | tf_op jit(solution)/shard_map/ppermute | solution.py:590
  39.6 18.1 %collective-permute-start.8 = (bf16[128,512]{1,0:T(8,128)(2,1)S(1)}, bf16[128,512]{1,0:T(8,128)(2,1)S(1)}, u32[]{:S(2)}, u32[]{:S(2)}) collective-permute-start(bf16[128,512]{1,0:T(8,128)(2,1)S(1)} %get-tuple-element.74), channel_id=1, source_target_pairs={{0,15},{1,0},{2,1},{3,2},{4,3},{5,4},{6,5},{7,6},{8,7},{9,8},{10,9... | collective-permute-start | bytes 393224 | tf_op jit(solution)/shard_map/ppermute | solution.py:590
  45.6 12.1 %collective-permute-start.11 = (bf16[128,512]{1,0:T(8,128)(2,1)S(1)}, bf16[128,512]{1,0:T(8,128)(2,1)S(1)}, u32[]{:S(2)}, u32[]{:S(2)}) collective-permute-start(bf16[128,512]{1,0:T(8,128)(2,1)S(1)} %get-tuple-element.78.refs_6_), channel_id=1, source_target_pairs={{0,16},{16,0},{32,48},{48,32},{64,80},{80,64},{96,112},{112,96},{1... | collective-permute-start | bytes 393224 | tf_op jit(solution)/shard_map/ppermute | solution.py:597
  49.9 9.3 %collective-permute-start.12 = (bf16[128,512]{1,0:T(8,128)(2,1)S(1)}, bf16[128,512]{1,0:T(8,128)(2,1)S(1)}, u32[]{:S(2)}, u32[]{:S(2)}) collective-permute-start(bf16[128,512]{1,0:T(8,128)(2,1)S(1)} %get-tuple-element.79), channel_id=1, source_target_pairs={{16,32},{48,64},{80,96},{32,16},{64,48},{96,80},{17,33},{49,65},{8... | collective-permute-start | bytes 393224 | tf_op jit(solution)/shard_map/ppermute | solution.py:596
  52.4 5.2 %collective-permute-start.6 = (bf16[16,256]{1,0:T(8,128)(2,1)S(1)}, bf16[16,256]{1,0:T(8,128)(2,1)S(1)}, u32[]{:S(2)}, u32[]{:S(2)}) collective-permute-start(bf16[16,256]{1,0:T(8,128)(2,1)S(1)} %get-tuple-element.69.refs_1_), channel_id=1, source_target_pairs={{0,64},{1,65},{2,66},{3,67},{4,68},{5,69},{6,70},{7,71},{8,72},{9,... | collective-permute-start | bytes 24584 | tf_op jit(solution)/shard_map/ppermute | solution.py:794
  60.8 7.2 %collective-permute-start.13 = (bf16[128,512]{1,0:T(8,128)(2,1)S(1)}, bf16[128,512]{1,0:T(8,128)(2,1)S(1)}, u32[]{:S(2)}, u32[]{:S(2)}) collective-permute-start(bf16[128,512]{1,0:T(8,128)(2,1)S(1)} %get-tuple-element.85.refs_3_.refs_1_), channel_id=1, source_target_pairs={{0,16},{16,0},{32,48},{48,32},{64,80},{80,64},{96,112},{112,96},{1... | collective-permute-start | bytes 393224 | tf_op jit(solution)/shard_map/ppermute | solution.py:816
  60.9 7.1 %collective-permute-start.14 = (bf16[16,512]{1,0:T(8,128)(2,1)S(1)}, bf16[16,512]{1,0:T(8,128)(2,1)S(1)}, u32[]{:S(2)}, u32[]{:S(2)}) collective-permute-start(bf16[16,512]{1,0:T(8,128)(2,1)S(1)} %get-tuple-element.86.refs_0_), channel_id=1, source_target_pairs={{0,2},{1,3},{2,0},{3,1},{4,6},{5,7},{6,4},{7,5},{8,10},{9,11},{10,... | collective-permute-start | bytes 49160 | tf_op jit(solution)/shard_map/ppermute | solution.py:817
  62.0 6.0 %collective-permute-start.15 = (bf16[16,512]{1,0:T(8,128)(2,1)S(1)}, bf16[16,512]{1,0:T(8,128)(2,1)S(1)}, u32[]{:S(2)}, u32[]{:S(2)}) collective-permute-start(bf16[16,512]{1,0:T(8,128)(2,1)S(1)} %get-tuple-element.86.refs_0_), channel_id=1, source_target_pairs={{0,18},{1,19},{2,16},{3,17},{4,22},{5,23},{6,20},{7,21},{8,26},{9,... | collective-permute-start | bytes 49160 | tf_op jit(solution)/shard_map/ppermute | solution.py:818
  68.0 11.0 %collective-permute-start.16 = (bf16[128,512]{1,0:T(8,128)(2,1)S(1)}, bf16[128,512]{1,0:T(8,128)(2,1)S(1)}, u32[]{:S(2)}, u32[]{:S(2)}) collective-permute-start(bf16[128,512]{1,0:T(8,128)(2,1)S(1)} %get-tuple-element.88.refs_2_), channel_id=1, source_target_pairs={{0,32},{16,48},{32,64},{48,80},{64,96},{80,112},{96,0},{112,16},{1... | collective-permute-start | bytes 393224 | tf_op jit(solution)/shard_map/ppermute | solution.py:838
  68.3 10.8 %collective-permute-start.17 = (bf16[128,512]{1,0:T(8,128)(2,1)S(1)}, bf16[128,512]{1,0:T(8,128)(2,1)S(1)}, u32[]{:S(2)}, u32[]{:S(2)}) collective-permute-start(bf16[128,512]{1,0:T(8,128)(2,1)S(1)} %get-tuple-element.88.refs_2_), channel_id=1, source_target_pairs={{0,96},{16,112},{32,0},{48,16},{64,32},{80,48},{96,64},{112,80},{1... | collective-permute-start | bytes 393224 | tf_op jit(solution)/shard_map/ppermute | solution.py:839
  71.3 7.0 %collective-permute-start.18 = (bf16[64,512]{1,0:T(8,128)(2,1)S(1)}, bf16[64,512]{1,0:T(8,128)(2,1)S(1)}, u32[]{:S(2)}, u32[]{:S(2)}) collective-permute-start(bf16[64,512]{1,0:T(8,128)(2,1)S(1)} %get-tuple-element.89.refs_5_), channel_id=1, source_target_pairs={{0,4},{1,5},{2,6},{3,7},{4,8},{5,9},{6,10},{7,11},{8,12},{9,13},{1... | collective-permute-start | bytes 196616 | tf_op jit(solution)/shard_map/ppermute | solution.py:837
  72.7 5.8 %collective-permute-start.19 = (bf16[64,512]{1,0:T(8,128)(2,1)S(1)}, bf16[64,512]{1,0:T(8,128)(2,1)S(1)}, u32[]{:S(2)}, u32[]{:S(2)}) collective-permute-start(bf16[64,512]{1,0:T(8,128)(2,1)S(1)} %get-tuple-element.89.refs_5_), channel_id=1, source_target_pairs={{0,8},{1,9},{2,10},{3,11},{4,12},{5,13},{6,14},{7,15},{8,0},{9,1},... | collective-permute-start | bytes 196616 | tf_op jit(solution)/shard_map/ppermute | solution.py:837
  74.8 4.3 %collective-permute-start.20 = (bf16[64,512]{1,0:T(8,128)(2,1)S(1)}, bf16[64,512]{1,0:T(8,128)(2,1)S(1)}, u32[]{:S(2)}, u32[]{:S(2)}) collective-permute-start(bf16[64,512]{1,0:T(8,128)(2,1)S(1)} %get-tuple-element.89.refs_5_), channel_id=1, source_target_pairs={{0,12},{1,13},{2,14},{3,15},{4,0},{5,1},{6,2},{7,3},{8,4},{9,5},{1... | collective-permute-start | bytes 196616 | tf_op jit(solution)/shard_map/ppermute | solution.py:837
  79.6 16.9 %collective-permute-start.21 = (bf16[3,128,512]{2,1,0:T(8,128)(2,1)S(1)}, bf16[3,128,512]{2,1,0:T(8,128)(2,1)S(1)}, u32[]{:S(2)}, u32[]{:S(2)}) collective-permute-start(bf16[3,128,512]{2,1,0:T(8,128)(2,1)S(1)} %get-tuple-element.91.refs_2_), channel_id=1, source_target_pairs={{0,1},{1,2},{2,3},{3,4},{4,5},{5,6},{6,7},{7,8},{8,9},{9,10},{10,1... | collective-permute-start | bytes 1179656 | tf_op jit(solution)/shard_map/ppermute | solution.py:590
  79.7 15.4 %collective-permute-start.23 = (bf16[256,512]{1,0:T(8,128)(2,1)S(1)}, bf16[256,512]{1,0:T(8,128)(2,1)S(1)}, u32[]{:S(2)}, u32[]{:S(2)}) collective-permute-start(bf16[256,512]{1,0:T(8,128)(2,1)S(1)} %get-tuple-element.93.refs_3_), channel_id=1, source_target_pairs={{0,32},{16,48},{32,64},{48,80},{64,96},{80,112},{96,0},{112,16},{1... | collective-permute-start | bytes 786440 | tf_op jit(solution)/shard_map/ppermute | solution.py:848
  79.8 15.8 %collective-permute-start.24 = (bf16[256,512]{1,0:T(8,128)(2,1)S(1)}, bf16[256,512]{1,0:T(8,128)(2,1)S(1)}, u32[]{:S(2)}, u32[]{:S(2)}) collective-permute-start(bf16[256,512]{1,0:T(8,128)(2,1)S(1)} %get-tuple-element.93.refs_3_), channel_id=1, source_target_pairs={{0,64},{16,80},{32,96},{48,112},{64,0},{80,16},{96,32},{112,48},{1... | collective-permute-start | bytes 786440 | tf_op jit(solution)/shard_map/ppermute | solution.py:848
  81.3 15.1 %collective-permute-start.25 = (bf16[256,512]{1,0:T(8,128)(2,1)S(1)}, bf16[256,512]{1,0:T(8,128)(2,1)S(1)}, u32[]{:S(2)}, u32[]{:S(2)}) collective-permute-start(bf16[256,512]{1,0:T(8,128)(2,1)S(1)} %get-tuple-element.93.refs_3_), channel_id=1, source_target_pairs={{0,96},{16,112},{32,0},{48,16},{64,32},{80,48},{96,64},{112,80},{1... | collective-permute-start | bytes 786440 | tf_op jit(solution)/shard_map/ppermute | solution.py:848
  83.0 13.8 %collective-permute-start.22 = (bf16[3,128,512]{2,1,0:T(8,128)(2,1)S(1)}, bf16[3,128,512]{2,1,0:T(8,128)(2,1)S(1)}, u32[]{:S(2)}, u32[]{:S(2)}) collective-permute-start(bf16[3,128,512]{2,1,0:T(8,128)(2,1)S(1)} %get-tuple-element.91.refs_2_), channel_id=1, source_target_pairs={{0,15},{1,0},{2,1},{3,2},{4,3},{5,4},{6,5},{7,6},{8,7},{9,8},{10,9... | collective-permute-start | bytes 1179656 | tf_op jit(solution)/shard_map/ppermute | solution.py:590
  101.3 9.2 %collective-permute-start.32 = (bf16[128,512]{1,0:T(8,128)(2,1)S(1)}, bf16[128,512]{1,0:T(8,128)(2,1)S(1)}, u32[]{:S(2)}, u32[]{:S(2)}) collective-permute-start(bf16[128,512]{1,0:T(8,128)(2,1)S(1)} %mesh.1.refs_3_.refs_2_), channel_id=1, source_target_pairs={{0,16},{16,0},{32,48},{48,32},{64,80},{80,64},{96,112},{112,96},{1... | collective-permute-start | bytes 393224 | tf_op jit(solution)/shard_map/ppermute | solution.py:597
  102.7 10.7 %collective-permute-start.33 = (bf16[128,512]{1,0:T(8,128)(2,1)S(1)}, bf16[128,512]{1,0:T(8,128)(2,1)S(1)}, u32[]{:S(2)}, u32[]{:S(2)}) collective-permute-start(bf16[128,512]{1,0:T(8,128)(2,1)S(1)} %mesh.1.refs_3_.refs_2_), channel_id=1, source_target_pairs={{16,32},{48,64},{80,96},{32,16},{64,48},{96,80},{17,33},{49,65},{8... | collective-permute-start | bytes 393224 | tf_op jit(solution)/shard_map/ppermute | solution.py:596
  106.5 11.3 %collective-permute-start.30 = (bf16[128,512]{1,0:T(8,128)(2,1)S(1)}, bf16[128,512]{1,0:T(8,128)(2,1)S(1)}, u32[]{:S(2)}, u32[]{:S(2)}) collective-permute-start(bf16[128,512]{1,0:T(8,128)(2,1)S(1)} %mesh.1.refs_3_.refs_2_), channel_id=1, source_target_pairs={{0,1},{1,2},{2,3},{3,4},{4,5},{5,6},{6,7},{7,8},{8,9},{9,10},{10,1... | collective-permute-start | bytes 393224 | tf_op jit(solution)/shard_map/ppermute | solution.py:590
  106.6 11.3 %collective-permute-start.31 = (bf16[128,512]{1,0:T(8,128)(2,1)S(1)}, bf16[128,512]{1,0:T(8,128)(2,1)S(1)}, u32[]{:S(2)}, u32[]{:S(2)}) collective-permute-start(bf16[128,512]{1,0:T(8,128)(2,1)S(1)} %mesh.1.refs_3_.refs_2_), channel_id=1, source_target_pairs={{0,15},{1,0},{2,1},{3,2},{4,3},{5,4},{6,5},{7,6},{8,7},{9,8},{10,9... | collective-permute-start | bytes 393224 | tf_op jit(solution)/shard_map/ppermute | solution.py:590
  113.9 8.5 %collective-permute-start.34 = (bf16[2,128,512]{2,1,0:T(8,128)(2,1)S(1)}, bf16[2,128,512]{2,1,0:T(8,128)(2,1)S(1)}, u32[]{:S(2)}, u32[]{:S(2)}) collective-permute-start(bf16[2,128,512]{2,1,0:T(8,128)(2,1)S(1)} %pair.3.refs_4_), channel_id=1, source_target_pairs={{0,1},{1,2},{2,3},{3,4},{4,5},{5,6},{6,7},{7,8},{8,9},{9,10},{10,1... | collective-permute-start | bytes 786440 | tf_op jit(solution)/shard_map/ppermute | solution.py:590
  114.0 8.4 %collective-permute-start.35 = (bf16[2,128,512]{2,1,0:T(8,128)(2,1)S(1)}, bf16[2,128,512]{2,1,0:T(8,128)(2,1)S(1)}, u32[]{:S(2)}, u32[]{:S(2)}) collective-permute-start(bf16[2,128,512]{2,1,0:T(8,128)(2,1)S(1)} %pair.3.refs_4_), channel_id=1, source_target_pairs={{0,15},{1,0},{2,1},{3,2},{4,3},{5,4},{6,5},{7,6},{8,7},{9,8},{10,9... | collective-permute-start | bytes 786440 | tf_op jit(solution)/shard_map/ppermute | solution.py:590
  (5 other events, 15.5 us)
